TPU v7x, 128 devices: a whole 4x4x4 slice. The times are simulated.
128 devices in a mesh: seq: 16 (over y_lo, x, core), dp: 8 (over z, y_hi).
Axes of the slice: x: 4, y: 4 (y_hi: 2, y_lo: 2; y = y_hi * 2 + y_lo), z: 4, core: 2. Of those that a mesh axis runs over, the one named last changes fastest.
Arguments:
- hidden: bfloat16 [8, 2048, 2048], P('dp', 'seq'), may hold values from -6 to 6
- short_taps: bfloat16 [4, 2048], replicated, may hold values from -3 to 3
- long_taps: bfloat16 [256, 16], replicated, may hold values from -0.375 to 0.375
- gate_weight: bfloat16 [2048, 2048], replicated, may hold values from -0.125 to 0.125
- upstream: bfloat16 [8, 2048, 2048], P('dp', 'seq'), may hold values from -6 to 6
Outputs:
- mixed_out: bfloat16 [8, 2048, 2048], P('dp', 'seq')
- grad_gate: float32 [2048, 2048], P(('seq', 'dp'))
- grad_short: float32 [4, 2048], replicated
- grad_long: float32 [256, 16], replicated
- d_hidden: bfloat16 [8, 2048, 2048], P('dp', 'seq')
All inputs are finite; a program needn't handle non-finite values.
Results may differ from a plain program's by a relative error of at most 0.0065.
Values may be sent and summed in bfloat16 or wider, within the bound.
A program may use at most 128 MiB of HBM per device.

v0:
```python
import jax
import jax.numpy as jnp
from jax import lax
from jax.sharding import PartitionSpec as P


def passed_along(value, axis, steps):
    count = lax.axis_size(axis)
    leading, last = (max(0, -steps), min(count, count - steps))
    return lax.ppermute(value, axis, [(source, source + steps) for source in range(leading, last)])


def swapped(block, axis, apart):
    count = lax.axis_size(axis)
    route = []
    for low in range(count):
        high = low | 1 << apart
        if high != low and high < count:
            route += [(low, high), (high, low)]
    return lax.ppermute(block, axis, route)


def short_causal(extended, short_taps, row_count):
    short_len = short_taps.shape[0]
    partial_sum = jnp.zeros((extended.shape[0], row_count, extended.shape[2]), jnp.float32)
    for tap_index in range(short_len):
        start_row = short_len - 1 - tap_index
        partial_sum = partial_sum + short_taps[tap_index].astype(jnp.float32) * extended[
            :, start_row : start_row + row_count
        ].astype(jnp.float32)
    return partial_sum


def band_matrix(long_taps, reverse):
    long_len, group_count = long_taps.shape
    block_size = long_len // 2
    taps_by_group = jnp.transpose(long_taps)
    if reverse:
        padded = jnp.concatenate(
            [
                jnp.zeros((group_count, block_size), long_taps.dtype),
                taps_by_group,
                jnp.zeros((group_count, block_size), long_taps.dtype),
            ],
            axis=1,
        )
    else:
        padded = jnp.concatenate(
            [
                jnp.zeros((group_count, block_size + 1), long_taps.dtype),
                jnp.flip(taps_by_group, 1),
                jnp.zeros((group_count, block_size - 1), long_taps.dtype),
            ],
            axis=1,
        )
    rolled = jnp.roll(padded, -block_size, axis=1)
    width = 4 * block_size
    tiled = jnp.tile(rolled, (1, block_size))[:, : block_size * (width - 1)]
    skewed = tiled.reshape(group_count, block_size, width - 1)
    return skewed[:, :, : 3 * block_size]


def band_apply(banded, extended, row_count):
    group_count, block_size = (banded.shape[0], banded.shape[1])
    block_count = row_count // block_size
    strands, channels = (extended.shape[0], extended.shape[2])
    tile_grid = extended.reshape(
        strands, block_count + 2, block_size, group_count, channels // group_count
    )
    partial_sum = jnp.zeros(
        (strands, block_count, block_size, group_count, channels // group_count), jnp.float32
    )
    for part_index in range(3):
        partial_sum = partial_sum + jnp.einsum(
            "gij,snjgc->snigc",
            banded[:, :, part_index * block_size : (part_index + 1) * block_size],
            tile_grid[:, part_index : part_index + block_count],
            preferred_element_type=jnp.float32,
        )
    return partial_sum.reshape(strands, row_count, channels)


def lag_sums(d_long, extended, long_len, group_count):
    strands, row_count, channels = d_long.shape
    block_size = long_len // 2
    block_count = row_count // block_size
    grad_tiles = d_long.reshape(
        strands, block_count, block_size, group_count, channels // group_count
    )
    input_tiles = extended.reshape(
        strands, block_count + 2, block_size, group_count, channels // group_count
    )
    products = [
        jnp.einsum(
            "snigc,snjgc->gij",
            grad_tiles,
            input_tiles[:, part_index : part_index + block_count],
            preferred_element_type=jnp.float32,
        )
        for part_index in range(3)
    ]
    joined = jnp.concatenate(products, axis=2).reshape(group_count, block_size * 3 * block_size)
    joined = jnp.pad(joined, ((0, 0), (0, block_size))).reshape(
        group_count, block_size, 3 * block_size + 1
    )
    diagonal = jnp.sum(joined, axis=1)
    return jnp.transpose(diagonal[:, 1 : 2 * block_size + 1][:, ::-1])


def strand_neighbour(rim_piece, offset):
    return passed_along(rim_piece, "seq", offset)


def fetch_mirrored(hidden, upstream):
    for bit_index in range(lax.axis_size("seq").bit_length() - 1):
        hidden, upstream = swapped((hidden, upstream), "seq", bit_index)
    return (hidden, upstream)


def mirror_pair(lead_piece, tail_piece):
    for bit_index in range(lax.axis_size("seq").bit_length() - 1):
        lead_piece, tail_piece = swapped((lead_piece, tail_piece), "seq", bit_index)
    return (lead_piece, tail_piece)


def body(hidden, short_taps, long_taps, gate_weight, upstream):
    row_count = hidden.shape[1]
    short_len = short_taps.shape[0]
    long_len, group_count = long_taps.shape
    channels = hidden.shape[2]
    rim_depth = (long_len - 2) // row_count + 1
    far_hidden, far_upstream = fetch_mirrored(hidden, upstream)
    reverse_in = jnp.flip(far_hidden[0], (0, 1))
    reverse_up = jnp.flip(far_upstream[0], (0, 1))
    strand_in = jnp.stack([hidden[0], reverse_in])
    prev_rim = strand_neighbour(strand_in[:, row_count - short_len + 1 :], 1)
    x_ext = jnp.concatenate([prev_rim, strand_in], axis=1)
    short_out = short_causal(x_ext, short_taps, row_count).astype(jnp.bfloat16)
    tail_rows = []
    for hop_count in range(1, rim_depth + 1):
        needed = min(row_count, long_len - 1 - (hop_count - 1) * row_count)
        tail_rows.insert(0, strand_neighbour(short_out[:, row_count - needed :], hop_count))
    zero_row = jnp.zeros((2, 1, channels), jnp.bfloat16)
    short_ext = jnp.concatenate([zero_row] + tail_rows + [short_out], axis=1)
    long_out = band_apply(band_matrix(long_taps, False), short_ext, row_count)
    gate_pre = jnp.einsum("srd,de->sre", strand_in, gate_weight, preferred_element_type=jnp.float32)
    sigmoid_gate = jax.nn.sigmoid(gate_pre)
    gated = (gate_pre * sigmoid_gate * long_out).astype(jnp.bfloat16)
    d_gated = jnp.stack([upstream[0], reverse_up])
    d_float = d_gated.astype(jnp.float32)
    d_long = (d_float * gate_pre * sigmoid_gate).astype(jnp.bfloat16)
    d_gate = (d_float * long_out * sigmoid_gate * (1.0 + gate_pre * (1.0 - sigmoid_gate))).astype(
        jnp.bfloat16
    )
    head_rows = []
    for hop_count in range(1, rim_depth + 1):
        needed = min(row_count, long_len - 1 - (hop_count - 1) * row_count)
        head_rows.append(strand_neighbour(d_long[:, :needed], -hop_count))
    d_ext = jnp.concatenate([d_long] + head_rows + [zero_row], axis=1)
    d_short = band_apply(band_matrix(long_taps, True), d_ext, row_count).astype(jnp.bfloat16)
    lag_term = lag_sums(d_long, short_ext, long_len, group_count)
    next_first = strand_neighbour(d_short[:, : short_len - 1], -1)
    d_short_ext = jnp.concatenate([d_short, next_first], axis=1)
    d_short_float = d_short.astype(jnp.float32)
    dx_short = jnp.zeros((2, row_count, channels), jnp.float32)
    short_rows = []
    for tap_index in range(short_len):
        dx_short = dx_short + short_taps[tap_index].astype(jnp.float32) * d_short_ext[
            :, tap_index : tap_index + row_count
        ].astype(jnp.float32)
        start_row = short_len - 1 - tap_index
        short_rows.append(
            jnp.sum(
                d_short_float * x_ext[:, start_row : start_row + row_count].astype(jnp.float32),
                axis=(0, 1),
            )
        )
    short_term = jnp.stack(short_rows)
    d_input = (
        jnp.einsum("sre,de->srd", d_gate, gate_weight, preferred_element_type=jnp.float32)
        + dx_short
    ).astype(jnp.bfloat16)
    far_gated, far_input = mirror_pair(gated[1:2], d_input[1:2])
    mixed_out = (
        gated[0].astype(jnp.float32) + jnp.flip(far_gated[0], (0, 1)).astype(jnp.float32)
    ).astype(jnp.bfloat16)
    d_hidden = (
        d_input[0].astype(jnp.float32) + jnp.flip(far_input[0], (0, 1)).astype(jnp.float32)
    ).astype(jnp.bfloat16)
    flat_input = strand_in.reshape(2 * row_count, channels)
    flat_gate = d_gate.reshape(2 * row_count, channels)
    grad_gate = lax.psum_scatter(
        jnp.einsum("tr,tc->rc", flat_input, flat_gate, preferred_element_type=jnp.float32),
        ("seq", "dp"),
        scatter_dimension=0,
        tiled=True,
    )
    grad_short, grad_long = lax.psum((short_term, lag_term), ("seq", "dp"))
    return (mixed_out[None], grad_gate, grad_short, grad_long, d_hidden[None])


def solution(mesh):
    placed = (P("dp", "seq", None), P(), P(), P(), P("dp", "seq", None))
    return jax.shard_map(
        body,
        mesh=mesh,
        in_specs=placed,
        out_specs=(P("dp", "seq", None), P(("seq", "dp"), None), P(), P(), P("dp", "seq", None)),
        check_vma=False,
    )
```

profile of v0, /device:TPU:1, one launch (start us, length us, event | category | flops | bytes accessed | tf_op | source)
XLA Modules:
  0.0 875.4 jit_solution(6582423562702535306)
XLA Ops:
  7.2 1.5 collective-permute-start
  8.7 1.7 collective-permute-done
  11.8 11.8 %collective-permute-done.1 = bf16[1,128,2048]{2,1,0:T(8,128)(2,1)S(1)} collective-permute-done((bf16[1,128,2048]{2,1,0:T(8,128)(2,1)S(1)}, bf16[1,128,2048]{2,1,0:T(8,128)(2,1)S(1)}, u32[]{:S(2)}, u32[]{:S(2)}) %collective-permute-start.1) | collective-permute-done | bytes 524320 | tf_op jit(solution)/shard_map/ppermute | solution.py:20
  23.6 2.8 collective-permute-start.2
  26.4 1.5 collective-permute-start.11
  27.9 9.4 %collective-permute-done.2 = bf16[1,128,2048]{2,1,0:T(8,128)(2,1)S(1)} collective-permute-done((bf16[1,128,2048]{2,1,0:T(8,128)(2,1)S(1)}, bf16[1,128,2048]{2,1,0:T(8,128)(2,1)S(1)}, u32[]{:S(2)}, u32[]{:S(2)}) %collective-permute-start.2) | collective-permute-done | bytes 524320 | tf_op jit(solution)/shard_map/ppermute | solution.py:20
  39.9 8.8 %collective-permute-done.3 = bf16[1,128,2048]{2,1,0:T(8,128)(2,1)S(1)} collective-permute-done((bf16[1,128,2048]{2,1,0:T(8,128)(2,1)S(1)}, bf16[1,128,2048]{2,1,0:T(8,128)(2,1)S(1)}, u32[]{:S(2)}, u32[]{:S(2)}) %collective-permute-start.3) | collective-permute-done | bytes 524320 | tf_op jit(solution)/shard_map/ppermute | solution.py:20
  48.7 1.8 rev.20
  51.3 6.0 collective-permute-start.4
  57.4 2.5 collective-permute-start.13
  61.2 2.6 collective-permute-start.6
  64.1 2.0 copy.45
  66.1 4.1 collective-permute-start.5
  70.2 2.1 collective-permute-done.13
  72.3 1.9 collective-permute-start.14
  75.8 1.5 slice.170
  77.4 5.9 reshape.152
  83.3 32.9 %collective-permute-done.14 = bf16[1,128,2048]{2,1,0:T(8,128)(2,1)} collective-permute-done((bf16[1,128,2048]{2,1,0:T(8,128)(2,1)}, bf16[1,128,2048]{2,1,0:T(8,128)(2,1)}, u32[]{:S(2)}, u32[]{:S(2)}) %collective-permute-start.14) | collective-permute-done | bytes 524320 | tf_op jit(solution)/shard_map/ppermute | solution.py:20
  116.2 8.8 %rev.23 = bf16[128,2048]{1,0:T(8,128)(2,1)} reverse(bf16[128,2048]{1,0:T(8,128)(2,1)} %bitcast.22), dimensions={0,1} | reverse | bytes 1048576 | tf_op jit(solution)/shard_map/jit(_flip)/rev | solution.py:134
  125.0 1.6 copy.46
  126.6 1.5 pad_maximum_fusion
  129.1 1.9 fusion.50
  131.0 2.4 copy.83
  133.4 1.6 copy.82
  135.0 1.7 copy.81
  136.8 2.2 fusion.35
  140.5 1.8 add_bitcast_fusion
  142.2 3.1 copy.50
  145.3 2.7 reshape.155
  148.0 8.4 fusion.10
  157.5 8.2 convolution_bitcast_fusion
  165.7 2.5 collective-permute-start.15
  168.3 2.1 copy.52
  174.0 1.5 slice.180
  175.5 6.0 reshape.158
  182.5 1.9 slice.177
  184.4 16.7 %collective-permute-done.16 = bf16[2,127,2048]{2,0,1:T(2,128)(2,1)} collective-permute-done((bf16[2,127,2048]{2,0,1:T(2,128)(2,1)}, bf16[2,127,2048]{2,0,1:T(2,128)(2,1)}, u32[]{:S(2)}, u32[]{:S(2)}) %collective-permute-start.16) | collective-permute-done | bytes 1040416 | tf_op jit(solution)/shard_map/ppermute | solution.py:10
  201.1 1.6 copy.53
  202.7 1.8 pad_maximum_fusion.1
  205.6 1.9 fusion.49
  207.5 1.7 copy.86
  209.2 2.4 copy.85
  211.6 2.4 copy.84
  214.1 1.9 fusion.28
  217.6 1.8 multiply_reduce_fusion
  219.4 2.7 copy.59
  222.0 1.5 convert_element_type.171
  223.6 10.9 %collective-permute-start.17 = (bf16[2,3,2048]{2,1,0:T(4,128)(2,1)S(1)}, bf16[2,3,2048]{2,1,0:T(4,128)(2,1)S(1)}, u32[]{:S(2)}, u32[]{:S(2)}) collective-permute-start(bf16[2,3,2048]{2,1,0:T(4,128)(2,1)S(1)} %slice.187), channel_id=1, source_target_pairs={{8,0},{16,8},{24,16},{32,24},{40,32},{48,40},{56,48},{64,56},{72,6... | collective-permute-start | bytes 73736 | tf_op jit(solution)/shard_map/ppermute | solution.py:10
  235.4 7.7 fusion.13
  243.4 1.8 collective-permute-done.18
  245.2 13.7 %collective-permute-done.8 = bf16[1,128,2048]{2,1,0:T(8,128)(2,1)S(1)} collective-permute-done((bf16[1,128,2048]{2,1,0:T(8,128)(2,1)}, bf16[1,128,2048]{2,1,0:T(8,128)(2,1)S(1)}, u32[]{:S(2)}, u32[]{:S(2)}) %collective-permute-start.8) | collective-permute-done | bytes 524320 | tf_op jit(solution)/shard_map/ppermute | solution.py:20
  258.9 4.8 collective-permute-start.9
  264.2 6.6 collective-permute-done.19
  270.8 6.2 collective-permute-start.20
  277.6 7.1 collective-permute-done.9
  285.4 2.5 copy.92
  287.8 2.1 pad.7
  290.0 4.6 reshape.163
  294.6 2.8 reduce_sum.49
  297.6 1.5 collective-permute-start.21
  299.2 91.0 %all-reduce.4 = (f32[4,2048]{1,0:T(4,128)}, f32[256,16]{0,1:T(8,128)}) all-reduce(f32[4,2048]{1,0:T(4,128)S(1)} %pad_maximum_fusion.7, f32[256,16]{0,1:T(8,128)S(1)} %bitcast.182), channel_id=1, replica_groups=mesh['seq'=16,'dp'=8] {'seq','dp'}, use_global_device_ids=true, to_apply=%region_5.6 | all-reduce | flops 12288 | bytes 98304 | tf_op jit(solution)/shard_map/psum | solution.py:198
  390.2 7.0 rev.22
  398.1 1.8 rev.25
  400.8 467.2 %reduce-scatter.2.cloned.1.call-done = f32[16,2048]{1,0:T(8,128)} async-done(((f32[2048,2048]{1,0:T(8,128)}), f32[16,2048]{1,0:T(8,128)}) %reduce-scatter.2.cloned.1.call-update) | async-done | bytes 131088 | tf_op jit(solution)/shard_map/reduce_scatter | solution.py:192
  (96 shorter events, 23.6 us)
Async XLA Ops:
  7.2 52.8 %copy-start = (bf16[1,128,2048]{2,1,0:T(8,128)(2,1)S(1)}, bf16[1,128,2048]{2,1,0:T(8,128)(2,1)}, u32[]{:S(2)}) copy-start(bf16[1,128,2048]{2,1,0:T(8,128)(2,1)} %param.5) | copy-start | bytes 1572868
  7.2 50.2 %copy-start.17 = (bf16[4,2048]{1,0:T(4,128)(2,1)S(1)}, bf16[4,2048]{1,0:T(4,128)(2,1)}, u32[]{:S(2)}) copy-start(bf16[4,2048]{1,0:T(4,128)(2,1)} %param.6) | copy-start | bytes 49156
  7.2 860.9 %reduce-scatter.2.cloned.1.call-start = ((), (), s32[]{:S(2)}) async-start(), calls=%async_computation.1 | async-start | bytes 16908288 | tf_op jit(solution)/shard_map/reduce_scatter | solution.py:192
  7.2 3.2 collective-permute-start
  10.5 13.1 %collective-permute-start.1 = (bf16[1,128,2048]{2,1,0:T(8,128)(2,1)S(1)}, bf16[1,128,2048]{2,1,0:T(8,128)(2,1)S(1)}, u32[]{:S(2)}, u32[]{:S(2)}) collective-permute-start(bf16[1,128,2048]{2,1,0:T(8,128)(2,1)S(1)} %collective-permute-done), channel_id=1, source_target_pairs={{0,16},{16,0},{8,24},{24,8},{32,48},{48,32},{40,56},{56,40},{64,80... | collective-permute-start | bytes 1572872 | tf_op jit(solution)/shard_map/ppermute | solution.py:20
  23.6 13.7 %collective-permute-start.2 = (bf16[1,128,2048]{2,1,0:T(8,128)(2,1)S(1)}, bf16[1,128,2048]{2,1,0:T(8,128)(2,1)S(1)}, u32[]{:S(2)}, u32[]{:S(2)}) collective-permute-start(bf16[1,128,2048]{2,1,0:T(8,128)(2,1)S(1)} %collective-permute-done.1), channel_id=1, source_target_pairs={{0,32},{32,0},{8,40},{40,8},{16,48},{48,16},{24,56},{56,24},{64,96... | collective-permute-start | bytes 1572872 | tf_op jit(solution)/shard_map/ppermute | solution.py:20
  26.4 12.3 %collective-permute-start.11 = (bf16[1,128,2048]{2,1,0:T(8,128)(2,1)}, bf16[1,128,2048]{2,1,0:T(8,128)(2,1)S(1)}, u32[]{:S(2)}, u32[]{:S(2)}) collective-permute-start(bf16[1,128,2048]{2,1,0:T(8,128)(2,1)} %param.9), channel_id=1, source_target_pairs={{0,8},{8,0},{16,24},{24,16},{32,40},{40,32},{48,56},{56,48},{64,72... | collective-permute-start | bytes 1572872 | tf_op jit(solution)/shard_map/ppermute | solution.py:20
  37.3 11.4 %collective-permute-start.3 = (bf16[1,128,2048]{2,1,0:T(8,128)(2,1)S(1)}, bf16[1,128,2048]{2,1,0:T(8,128)(2,1)S(1)}, u32[]{:S(2)}, u32[]{:S(2)}) collective-permute-start(bf16[1,128,2048]{2,1,0:T(8,128)(2,1)S(1)} %collective-permute-done.2), channel_id=1, source_target_pairs={{0,64},{64,0},{8,72},{72,8},{16,80},{80,16},{24,88},{88,24},{32,96... | collective-permute-start | bytes 1572872 | tf_op jit(solution)/shard_map/ppermute | solution.py:20
  38.7 18.7 %collective-permute-start.12 = (bf16[1,128,2048]{2,1,0:T(8,128)(2,1)S(1)}, bf16[1,128,2048]{2,1,0:T(8,128)(2,1)}, u32[]{:S(2)}, u32[]{:S(2)}) collective-permute-start(bf16[1,128,2048]{2,1,0:T(8,128)(2,1)S(1)} %collective-permute-done.11), channel_id=1, source_target_pairs={{0,16},{16,0},{8,24},{24,8},{32,48},{48,32},{40,56},{56,40},{64,80... | collective-permute-start | bytes 1572872 | tf_op jit(solution)/shard_map/ppermute | solution.py:20
  51.3 8.6 collective-permute-start.4
  57.4 14.9 %collective-permute-start.13 = (bf16[1,128,2048]{2,1,0:T(8,128)(2,1)}, bf16[1,128,2048]{2,1,0:T(8,128)(2,1)}, u32[]{:S(2)}, u32[]{:S(2)}) collective-permute-start(bf16[1,128,2048]{2,1,0:T(8,128)(2,1)} %collective-permute-done.12), channel_id=1, source_target_pairs={{0,32},{32,0},{8,40},{40,8},{16,48},{48,16},{24,56},{56,24},{64,96... | collective-permute-start | bytes 1572872 | tf_op jit(solution)/shard_map/ppermute | solution.py:20
  61.1 13.0 %copy-start.18 = (bf16[256,16]{0,1:T(8,128)(2,1)S(1)}, bf16[256,16]{0,1:T(8,128)(2,1)}, u32[]{:S(2)}) copy-start(bf16[256,16]{0,1:T(8,128)(2,1)} %param.7) | copy-start | bytes 24580
  61.2 65.4 %collective-permute-start.6 = (bf16[2,128,2048]{2,1,0:T(8,128)(2,1)S(1)}, bf16[2,128,2048]{2,1,0:T(8,128)(2,1)}, u32[]{:S(2)}, u32[]{:S(2)}) collective-permute-start(bf16[2,128,2048]{2,1,0:T(8,128)(2,1)S(1)} %fusion.7), channel_id=1, source_target_pairs={{0,8},{8,16},{16,24},{24,32},{32,40},{40,48},{48,56},{56,64},{64,7... | collective-permute-start | bytes 3145736 | tf_op jit(solution)/shard_map/ppermute | solution.py:10
  66.1 58.9 %collective-permute-start.5 = (bf16[2,127,2048]{2,0,1:T(2,128)(2,1)}, bf16[2,127,2048]{2,0,1:T(2,128)(2,1)}, u32[]{:S(2)}, u32[]{:S(2)}) collective-permute-start(bf16[2,127,2048]{2,0,1:T(2,128)(2,1)} %copy.45), channel_id=1, source_target_pairs={{0,16},{8,24},{16,32},{24,40},{32,48},{40,56},{48,64},{56,72},{64,... | collective-permute-start | bytes 3121160 | tf_op jit(solution)/shard_map/ppermute | solution.py:10
  72.3 43.9 %collective-permute-start.14 = (bf16[1,128,2048]{2,1,0:T(8,128)(2,1)}, bf16[1,128,2048]{2,1,0:T(8,128)(2,1)}, u32[]{:S(2)}, u32[]{:S(2)}) collective-permute-start(bf16[1,128,2048]{2,1,0:T(8,128)(2,1)} %collective-permute-done.13), channel_id=1, source_target_pairs={{0,64},{64,0},{8,72},{72,8},{16,80},{80,16},{24,88},{88,24},{32,96... | collective-permute-start | bytes 1572872 | tf_op jit(solution)/shard_map/ppermute | solution.py:20
  136.8 2.9 copy-start.1
  136.8 2.5 copy-start.7
  139.2 1.2 copy-start.3
  156.5 1.0 copy-start.12
  165.7 37.0 %collective-permute-start.15 = (bf16[2,128,2048]{2,1,0:T(8,128)(2,1)S(1)}, bf16[2,128,2048]{2,1,0:T(8,128)(2,1)}, u32[]{:S(2)}, u32[]{:S(2)}) collective-permute-start(bf16[2,128,2048]{2,1,0:T(8,128)(2,1)S(1)} %get-tuple-element.15), channel_id=1, source_target_pairs={{8,0},{16,8},{24,16},{32,24},{40,32},{48,40},{56,48},{64,56},{72,6... | collective-permute-start | bytes 3145736 | tf_op jit(solution)/shard_map/ppermute | solution.py:10
  170.4 30.8 %collective-permute-start.16 = (bf16[2,127,2048]{2,0,1:T(2,128)(2,1)}, bf16[2,127,2048]{2,0,1:T(2,128)(2,1)}, u32[]{:S(2)}, u32[]{:S(2)}) collective-permute-start(bf16[2,127,2048]{2,0,1:T(2,128)(2,1)} %copy.52), channel_id=1, source_target_pairs={{16,0},{24,8},{32,16},{40,24},{48,32},{56,40},{64,48},{72,56},{80,... | collective-permute-start | bytes 3121160 | tf_op jit(solution)/shard_map/ppermute | solution.py:10
  184.4 58.9 %collective-permute-start.7 = (bf16[1,128,2048]{2,1,0:T(8,128)(2,1)}, bf16[1,128,2048]{2,1,0:T(8,128)(2,1)}, u32[]{:S(2)}, u32[]{:S(2)}) collective-permute-start(bf16[1,128,2048]{2,1,0:T(8,128)(2,1)} %slice.177), channel_id=1, source_target_pairs={{0,8},{8,0},{16,24},{24,16},{32,40},{40,32},{48,56},{56,48},{64,72... | collective-permute-start | bytes 1572872 | tf_op jit(solution)/shard_map/ppermute | solution.py:20
  214.1 2.1 copy-start.6
  214.1 2.3 copy-start.9
  216.4 1.0 copy-start.10
  216.4 1.2 copy-start.11
  223.6 11.8 %copy-start.8 = (bf16[2,128,2048]{2,1,0:T(8,128)(2,1)}, bf16[2,128,2048]{2,1,0:T(8,128)(2,1)S(1)}, u32[]{:S(2)}) copy-start(bf16[2,128,2048]{2,1,0:T(8,128)(2,1)S(1)} %convert_element_type.171) | copy-start | bytes 3145732
  223.6 11.8 %copy-start.13 = (bf16[2,128,2048]{2,1,0:T(8,128)(2,1)S(1)}, bf16[2,128,2048]{2,1,0:T(8,128)(2,1)}, u32[]{:S(2)}) copy-start(bf16[2,128,2048]{2,1,0:T(8,128)(2,1)} %copy-done.12) | copy-start | bytes 3145732
  223.6 11.8 %collective-permute-start.17 = (bf16[2,3,2048]{2,1,0:T(4,128)(2,1)S(1)}, bf16[2,3,2048]{2,1,0:T(4,128)(2,1)S(1)}, u32[]{:S(2)}, u32[]{:S(2)}) collective-permute-start(bf16[2,3,2048]{2,1,0:T(4,128)(2,1)S(1)} %slice.187), channel_id=1, source_target_pairs={{8,0},{16,8},{24,16},{32,24},{40,32},{48,40},{56,48},{64,56},{72,6... | collective-permute-start | bytes 73736 | tf_op jit(solution)/shard_map/ppermute | solution.py:10
  235.4 28.3 %copy-start.5 = (bf16[2,1,128,16,128]{2,4,0,3,1:T(8,128)(2,1)S(1)}, bf16[2,1,128,16,128]{2,4,0,3,1:T(8,128)(2,1)}, u32[]{:S(2)}) copy-start(bf16[2,1,128,16,128]{2,4,0,3,1:T(8,128)(2,1)} %copy.82) | copy-start | bytes 3145732
  243.1 21.1 %copy-start.15 = (bf16[2,128,2048]{2,1,0:T(8,128)(2,1)}, bf16[2,128,2048]{2,1,0:T(8,128)(2,1)S(1)}, u32[]{:S(2)}) copy-start(bf16[2,128,2048]{2,1,0:T(8,128)(2,1)S(1)} %get-tuple-element.19) | copy-start | bytes 3145732
  243.1 33.9 %copy-start.4 = (bf16[2,1,128,16,128]{2,4,0,3,1:T(8,128)(2,1)S(1)}, bf16[2,1,128,16,128]{2,4,0,3,1:T(8,128)(2,1)}, u32[]{:S(2)}) copy-start(bf16[2,1,128,16,128]{2,4,0,3,1:T(8,128)(2,1)} %copy.83) | copy-start | bytes 3145732
  243.2 2.0 collective-permute-start.18
  243.3 15.6 %collective-permute-start.8 = (bf16[1,128,2048]{2,1,0:T(8,128)(2,1)}, bf16[1,128,2048]{2,1,0:T(8,128)(2,1)S(1)}, u32[]{:S(2)}, u32[]{:S(2)}) collective-permute-start(bf16[1,128,2048]{2,1,0:T(8,128)(2,1)} %collective-permute-done.7), channel_id=1, source_target_pairs={{0,16},{16,0},{8,24},{24,8},{32,48},{48,32},{40,56},{56,40},{64,80... | collective-permute-start | bytes 1572872 | tf_op jit(solution)/shard_map/ppermute | solution.py:20
  245.2 25.6 %collective-permute-start.19 = (bf16[1,128,2048]{2,1,0:T(8,128)(2,1)S(1)}, bf16[1,128,2048]{2,1,0:T(8,128)(2,1)}, u32[]{:S(2)}, u32[]{:S(2)}) collective-permute-start(bf16[1,128,2048]{2,1,0:T(8,128)(2,1)S(1)} %collective-permute-done.18), channel_id=1, source_target_pairs={{0,16},{16,0},{8,24},{24,8},{32,48},{48,32},{40,56},{56,40},{64,80... | collective-permute-start | bytes 1572872 | tf_op jit(solution)/shard_map/ppermute | solution.py:20
  258.9 25.8 %collective-permute-start.9 = (bf16[1,128,2048]{2,1,0:T(8,128)(2,1)S(1)}, bf16[1,128,2048]{2,1,0:T(8,128)(2,1)}, u32[]{:S(2)}, u32[]{:S(2)}) collective-permute-start(bf16[1,128,2048]{2,1,0:T(8,128)(2,1)S(1)} %collective-permute-done.8), channel_id=1, source_target_pairs={{0,32},{32,0},{8,40},{40,8},{16,48},{48,16},{24,56},{56,24},{64,96... | collective-permute-start | bytes 1572872 | tf_op jit(solution)/shard_map/ppermute | solution.py:20
  264.2 20.4 %copy-start.2 = (bf16[2,1,128,16,128]{2,4,0,3,1:T(8,128)(2,1)S(1)}, bf16[2,1,128,16,128]{2,4,0,3,1:T(8,128)(2,1)}, u32[]{:S(2)}) copy-start(bf16[2,1,128,16,128]{2,4,0,3,1:T(8,128)(2,1)} %copy-done.1) | copy-start | bytes 3145732
  270.8 26.8 %collective-permute-start.20 = (bf16[1,128,2048]{2,1,0:T(8,128)(2,1)}, bf16[1,128,2048]{2,1,0:T(8,128)(2,1)}, u32[]{:S(2)}, u32[]{:S(2)}) collective-permute-start(bf16[1,128,2048]{2,1,0:T(8,128)(2,1)} %collective-permute-done.19), channel_id=1, source_target_pairs={{0,32},{32,0},{8,40},{40,8},{16,48},{48,16},{24,56},{56,24},{64,96... | collective-permute-start | bytes 1572872 | tf_op jit(solution)/shard_map/ppermute | solution.py:20
  284.7 105.5 %collective-permute-start.10 = (bf16[1,128,2048]{2,1,0:T(8,128)(2,1)}, bf16[1,128,2048]{2,1,0:T(8,128)(2,1)}, u32[]{:S(2)}, u32[]{:S(2)}) collective-permute-start(bf16[1,128,2048]{2,1,0:T(8,128)(2,1)} %collective-permute-done.9), channel_id=1, source_target_pairs={{0,64},{64,0},{8,72},{72,8},{16,80},{80,16},{24,88},{88,24},{32,96... | collective-permute-start | bytes 1572872 | tf_op jit(solution)/shard_map/ppermute | solution.py:20
  294.6 102.6 %copy-start.14 = (bf16[2,128,2048]{2,1,0:T(8,128)(2,1)S(1)}, bf16[2,128,2048]{2,1,0:T(8,128)(2,1)}, u32[]{:S(2)}) copy-start(bf16[2,128,2048]{2,1,0:T(8,128)(2,1)} %get-tuple-element.11) | copy-start | bytes 3145732
  297.4 102.5 %copy-start.16 = (bf16[2,128,2048]{2,1,0:T(8,128)(2,1)S(1)}, bf16[2,128,2048]{2,1,0:T(8,128)(2,1)}, u32[]{:S(2)}) copy-start(bf16[2,128,2048]{2,1,0:T(8,128)(2,1)} %copy-done.15) | copy-start | bytes 3145732
  297.6 100.5 %collective-permute-start.21 = (bf16[1,128,2048]{2,1,0:T(8,128)(2,1)}, bf16[1,128,2048]{2,1,0:T(8,128)(2,1)S(1)}, u32[]{:S(2)}, u32[]{:S(2)}) collective-permute-start(bf16[1,128,2048]{2,1,0:T(8,128)(2,1)} %collective-permute-done.20), channel_id=1, source_target_pairs={{0,64},{64,0},{8,72},{72,8},{16,80},{80,16},{24,88},{88,24},{32,96... | collective-permute-start | bytes 1572872 | tf_op jit(solution)/shard_map/ppermute | solution.py:20
Sparse Core Ops, SparseCore 0:
  165.8 702.1 reduce-scatter.1
where the time goes:
time: 890 us; the launch traced here: 875 us
  waiting for transfers between devices  581 us (65%)
  blocking collectives  91 us (10%)
  local copies, waits for them, and re-layouts  89.5 us (10%)
  starting transfers between devices  54.3 us (6%)
  matrix products  34.3 us (4%)
  between operations  15 us (2%)
  other arithmetic  10.4 us (1%)
    reduce_scatter x1, waiting for transfers between devices, body(): lax.psum_scatter(jnp.einsum('tr,tc->rc', flat_input, flat_gate, preferred...  467 us
    ppermute x16, waiting for transfers between devices, swapped(): return lax.ppermute(block, axis, route)  96 us
    psum x1, blocking collectives, body(): grad_short, grad_long = lax.psum((short_term, lag_term), ('seq', 'dp'))  91 us
    ppermute x6, starting transfers between devices, passed_along(): lax.ppermute(value, axis, [(source, source + steps) for source in range(l...  27.5 us
    ppermute x16, starting transfers between devices, swapped(): return lax.ppermute(block, axis, route)  26.8 us
    unnamed x51, local copies, waits for them, and re-layouts  23.5 us
  transfers between devices with their start and end apart: 23, of which 13 were waited for; matrix products, arithmetic and copies ran while one was open for 11% of the time, Pallas kernels for 0%

commit v1 on v0

v1 whole, which is shorter than its diff:
```python
import types

import jax
import jax.numpy as jnp
from jax import lax
from jax.experimental import pallas as pl
from jax.experimental.pallas import tpu as pltpu
from jax.sharding import PartitionSpec as P

BF = jnp.bfloat16
F32 = jnp.float32
MESH = pl.DeviceIdType.MESH
NT = (((1,), (1,)), ((), ()))
TN = (((0,), (0,)), ((), ()))

WIDTHS = (256, 384, 384)
STARTS = (0, 256, 640)
RING = 4
SMALL = 1280

SCRATCH = dict(
    hh=((512, 2048), BF),
    w=((2048, 1024), BF),
    up=((256, 1024), BF),
    upj=((256, 1024), BF),
    halo=((2, 16, 2048), BF),
    st=((4, 2048), F32),
    xf=((272, 1024), BF),
    xr=((272, 1024), BF),
    sf=((512, 1024), BF),
    sr=((512, 1024), BF),
    df=((512, 1024), BF),
    dr=((512, 1024), BF),
    gate=((512, 1024), F32),
    gr=((512, 1024), BF),
    mx=((256, 1024), BF),
    dg=((512, 1024), BF),
    tt=((8, 256, 512), BF),
    uu=((8, 256, 512), BF),
    tv=((16, 512), F32),
    uv=((16, 512), F32),
    jm=((256, 256), BF),
    im=((256, 256), BF),
    xt=((2048, 512), BF),
    pa=((2, 4, 256, WIDTHS[0]), BF),
    pb=((2, 32, 2, 16, WIDTHS[1]), BF),
    pc=((16, 4, 32, WIDTHS[2]), BF),
    ra1=((3, 2, 256, WIDTHS[0]), BF),
    rb1=((3, 32, 16, WIDTHS[1]), BF),
    rc1=((3, 16, 32, WIDTHS[2]), BF),
    sa1=((2, 8, 2, 16, WIDTHS[0]), BF),
    sb1=((8, 4, 16, WIDTHS[1]), BF),
    sc1=((2, 4, 64, WIDTHS[2]), BF),
    ra2=((3, 8, 16, WIDTHS[0]), BF),
    rb2=((3, 8, 16, WIDTHS[1]), BF),
    rc2=((3, 2, 64, WIDTHS[2]), BF),
    sa2=((2, 4, 16, WIDTHS[0]), BF),
    sb2=((4, 32, WIDTHS[1]), BF),
    sc2=((2, 2, 2, 16, WIDTHS[2]), BF),
    ra3=((3, 2, 16, WIDTHS[0]), BF),
    rb3=((3, 32, WIDTHS[1]), BF),
    rc3=((3, 2, 16, WIDTHS[2]), BF),
    fin=((2, 16, 1024), F32),
    dsf=((272, 1024), BF),
    dsr=((272, 1024), BF),
    ls=((2, 8, 8, 512), F32),
    sm=((3, 4, 8, SMALL), F32),
    smo=((8, SMALL), F32),
    dh=((256, 2048), F32),
    dxr=((256, 1024), BF),
    dhs=((128, 2048), BF),
    dhr=((128, 2048), BF),
    dho=((128, 2048), BF),
)
LOCAL_SEMS = 16
REMOTE_SEMS = 64


def dot(a, b):
    return jnp.dot(a, b, preferred_element_type=F32)


def dot_nt(a, b):
    return lax.dot_general(a, b, NT, preferred_element_type=F32)


def skew_sum(m, to_left):
    rows, lanes = m.shape
    while rows > 8:
        rows //= 2
        shift = lanes - rows if to_left else rows
        m = m[:rows] + pltpu.roll(m[rows:], shift, 1)
    return m


def kernel(hidden, staps, ltaps, weight, upstream, mixed, ggate, small, dhid, *scratch):
    r = types.SimpleNamespace(**dict(zip(SCRATCH, scratch)))
    loc, send, recv = scratch[len(SCRATCH) :]

    seq, dp = lax.axis_index("seq"), lax.axis_index("dp")
    core = lax.rem(seq, 2)
    chip = seq // 2
    x = lax.rem(chip, 4)
    y_lo = chip // 4
    y_hi = lax.rem(dp, 2)
    y = y_hi * 2 + y_lo
    z = dp // 2
    other = 1 - core

    def at_chip(c, k):
        return {"seq": c * 2 + k, "dp": dp}

    def x_peer(o):
        return {"seq": (y_lo * 4 + lax.rem(x + o, 4)) * 2 + core, "dp": dp}

    def y_peer(o):
        t = lax.rem(y + o, 4)
        return {
            "seq": (lax.rem(t, 2) * 4 + x) * 2 + core,
            "dp": z * 2 + t // 2,
        }

    def z_peer(o):
        return {"seq": seq, "dp": lax.rem(z + o, 4) * 2 + y_hi}

    partner = at_chip(chip, other)
    nxt, prv = lax.rem(chip + 1, 8), lax.rem(chip + 7, 8)
    cross_chip = lax.rem(chip + 8 + 2 * core - 1, 8)
    peers = [partner, at_chip(nxt, core), at_chip(prv, core), at_chip(cross_chip, other)]
    peers += [f(o) for f in (x_peer, y_peer, z_peer) for o in (1, 2, 3)]

    offs = [pl.multiple_of(512 * other, 512), pl.multiple_of(1024 + 512 * core, 512)]
    offs_other = [pl.multiple_of(512 * core, 512), pl.multiple_of(1024 + 512 * other, 512)]
    own = pl.multiple_of(core * 128, 128)
    theirs = pl.multiple_of(other * 128, 128)

    def col(g, width):
        half = 512 // width
        c = jnp.where(g < half, 512 * other + g * width, 512 + 512 * core + g * width)
        return pl.multiple_of(c, width)

    started = []
    count = [0]

    def remote(src, dst, device, recv_index=None):
        i = count[0]
        count[0] += 1
        copy = pltpu.make_async_remote_copy(
            src_ref=src,
            dst_ref=dst,
            send_sem=send.at[i],
            recv_sem=recv.at[i if recv_index is None else recv_index],
            device_id=device,
            device_id_type=MESH,
        )
        copy.start()
        started.append(copy)
        return copy

    lcount = [0]

    def local(src, dst):
        copy = pltpu.make_async_copy(src, dst, loc.at[lcount[0]])
        lcount[0] += 1
        copy.start()
        return copy

    in_h = local(hidden.at[0], r.hh.at[pl.ds(own, 128)])
    in_u = [
        local(
            upstream.at[0, :, pl.ds(offs[i], 512)],
            r.up.at[pl.ds(own, 128), pl.ds(512 * i, 512)],
        )
        for i in range(2)
    ]
    in_w = [
        local(weight.at[:, pl.ds(offs[i], 512)], r.w.at[:, pl.ds(512 * i, 512)])
        for i in range(2)
    ]

    barrier = pltpu.get_barrier_semaphore()
    for peer in peers:
        pl.semaphore_signal(barrier, inc=1, device_id=peer, device_id_type=MESH)
    pl.semaphore_wait(barrier, len(peers))

    halo_base = REMOTE_SEMS - 2
    halo_src = hidden.at[0, pl.ds(pl.multiple_of(core * 112, 16), 16)]
    for k in range(2):
        halo_copy = remote(
            halo_src, r.halo.at[other], at_chip(cross_chip, k), halo_base + other
        )
    pair_h = remote(hidden.at[0], r.hh.at[pl.ds(own, 128)], partner)
    pair_u = [
        remote(
            upstream.at[0, :, pl.ds(offs_other[i], 512)],
            r.up.at[pl.ds(own, 128), pl.ds(512 * i, 512)],
            partner,
        )
        for i in range(2)
    ]

    rows_i = lax.broadcasted_iota(jnp.int32, (256, 256), 0)
    cols_i = lax.broadcasted_iota(jnp.int32, (256, 256), 1)
    r.jm[...] = jnp.where(rows_i + cols_i == 255, 1.0, 0.0).astype(BF)
    r.im[...] = jnp.where(rows_i == cols_i, 1.0, 0.0).astype(BF)
    r.st[...] = staps[...].astype(F32)

    tap_i = lax.broadcasted_iota(jnp.int32, (256, 512), 0)
    lag_i = lax.broadcasted_iota(jnp.int32, (256, 512), 1)
    taps = ltaps[...]
    r.tv[...] = lax.dot_general(
        taps,
        jnp.where(tap_i + lag_i == 256, 1.0, 0.0).astype(BF),
        TN,
        preferred_element_type=F32,
    )
    r.uv[...] = lax.dot_general(
        taps, jnp.where(tap_i == lag_i, 1.0, 0.0).astype(BF), TN, preferred_element_type=F32
    )

    def toeplitz(g, carry):
        gg = col(g, 128) // 128
        for vec, out in ((r.tv, r.tt), (r.uv, r.uu)):
            first = pltpu.roll(
                jnp.broadcast_to(vec[pl.ds(gg, 1), :], (32, 512)), 0, 1, stride=1, stride_axis=0
            )
            for b in range(8):
                block = first if b == 0 else pltpu.roll(first, 32 * b, 1)
                out[g, 32 * b : 32 * b + 32, :] = block.astype(BF)
        return carry

    lax.fori_loop(0, 8, toeplitz, 0)

    in_h.wait()
    pair_h.wait_recv()

    def flip_rows(i, carry):
        here = pl.multiple_of(i * 256, 256)
        there = pl.multiple_of(1792 - i * 256, 256)
        r.hh[256:512, pl.ds(here, 256)] = dot(r.hh[0:256, pl.ds(there, 256)], r.jm[...]).astype(BF)
        return carry

    lax.fori_loop(0, 8, flip_rows, 0)

    for k in range(2):
        pltpu.make_async_remote_copy(
            src_ref=halo_src,
            dst_ref=r.halo.at[k],
            send_sem=send.at[0],
            recv_sem=recv.at[halo_base + k],
            device_id=partner,
            device_id_type=MESH,
        ).wait_recv()

    @pl.when(chip == 0)
    def _():
        r.halo[0] = jnp.zeros((16, 2048), BF)

    @pl.when(chip == 7)
    def _():
        r.halo[1] = jnp.zeros((16, 2048), BF)

    for i in range(2):
        span = slice(512 * i, 512 * i + 512)
        r.xf[0:16, span] = r.halo[0, :, pl.ds(offs[i], 512)]
        r.xf[16:272, span] = r.hh[0:256, pl.ds(offs[i], 512)]
        r.xr[0:256, span] = r.hh[256:512, pl.ds(offs[i], 512)]
    for i in range(4):
        flipped = dot(r.halo[1, :, pl.ds(col(3 - i, 256), 256)], r.jm[...])
        r.xr[256:272, 256 * i : 256 * i + 256] = flipped.astype(BF)

    def short_conv(g, carry):
        here = pl.ds(pl.multiple_of(g * 128, 128), 128)
        there = pl.ds(col(g, 128), 128)
        fwd = r.xf[:, here].astype(F32)
        rev = r.xr[:, here].astype(F32)
        acc_f = r.st[0:1, there] * fwd[16:272]
        acc_r = r.st[0:1, there] * rev[0:256]
        for k in range(1, 4):
            tap = r.st[k : k + 1, there]
            acc_f += tap * pltpu.roll(fwd, k, 0)[16:272]
            acc_r += tap * pltpu.roll(rev, 272 - k, 0)[0:256]
        r.sf[256:512, here] = acc_f.astype(BF)
        r.sr[0:256, here] = acc_r.astype(BF)
        return carry

    lax.fori_loop(0, 8, short_conv, 0)
    rim_sf = remote(r.sf.at[pl.ds(256, 256)], r.sf.at[pl.ds(0, 256)], at_chip(nxt, core))
    rim_sr = remote(r.sr.at[pl.ds(0, 256)], r.sr.at[pl.ds(256, 256)], at_chip(prv, core))

    for copy in in_w + in_u:
        copy.wait()
    for copy in pair_u:
        copy.wait_recv()

    def gate_block(i, carry):
        here = pl.ds(pl.multiple_of(i * 256, 256), 256)
        there = pl.ds(pl.multiple_of(768 - i * 256, 256), 256)
        r.gate[:, here] = dot(r.hh[...], r.w[:, here])
        r.upj[:, here] = dot(r.up[:, there], r.jm[...]).astype(BF)

        def rows(b, carry):
            at = pl.multiple_of(b * 32, 32)
            gf = r.gate[pl.ds(at, 32), here]
            gb = r.gate[pl.ds(at + 256, 32), here]
            uf = r.up[pl.ds(at, 32), here].astype(F32)
            ub = r.upj[pl.ds(at, 32), here].astype(F32)
            r.df[pl.ds(at, 32), here] = (uf * gf * jax.nn.sigmoid(gf)).astype(BF)
            r.dr[pl.ds(at + 256, 32), here] = (ub * gb * jax.nn.sigmoid(gb)).astype(BF)
            return carry

        return lax.fori_loop(0, 8, rows, carry)

    lax.fori_loop(0, 4, gate_block, 0)
    rim_df = remote(r.df.at[pl.ds(0, 256)], r.df.at[pl.ds(256, 256)], at_chip(prv, core))
    rim_dr = remote(r.dr.at[pl.ds(256, 256)], r.dr.at[pl.ds(0, 256)], at_chip(nxt, core))

    def transposed(i, carry):
        here = pl.ds(pl.multiple_of(i * 256, 256), 256)
        r.xt[here, 0:256] = dot_nt(r.im[...], r.hh[0:256, here]).astype(BF)
        r.xt[here, 256:512] = dot_nt(r.im[...], r.hh[256:512, here]).astype(BF)
        return carry

    lax.fori_loop(0, 8, transposed, 0)

    rim_sf.wait_recv()
    rim_sr.wait_recv()

    @pl.when(chip == 0)
    def _():
        r.sf[0:256, :] = jnp.zeros((256, 1024), BF)

    @pl.when(chip == 7)
    def _():
        r.sr[256:512, :] = jnp.zeros((256, 1024), BF)

    def long_conv(g, carry):
        here = pl.ds(pl.multiple_of(g * 128, 128), 128)
        for base, mat, inp, upref in ((0, r.tt, r.sf, r.up), (256, r.uu, r.sr, r.upj)):
            long_out = dot(mat[g], inp[:, here])
            g_pre = r.gate[base : base + 256, here]
            s = jax.nn.sigmoid(g_pre)
            ul = upref[:, here].astype(F32) * long_out
            r.gr[base : base + 256, here] = (g_pre * s * long_out).astype(BF)
            r.dg[base : base + 256, here] = (ul * s * (1.0 + g_pre * (1.0 - s))).astype(BF)
        return carry

    lax.fori_loop(0, 8, long_conv, 0)

    first, c_b, w_b = [], STARTS[1], WIDTHS[1]

    def part_b(i, carry):
        blk = dot(r.xt[pl.ds(pl.multiple_of(i * 256, 256), 256), :], r.dg[:, c_b : c_b + w_b])
        r.pb[i // 4, pl.ds(lax.rem(i, 4) * 8, 8)] = blk.astype(BF).reshape(8, 2, 16, w_b)
        return carry

    def part_c(i, carry):
        c, w = STARTS[2], WIDTHS[2]
        blk = dot(r.xt[pl.ds(pl.multiple_of(i * 256, 256), 256), :], r.dg[:, c : c + w])
        r.pc[pl.ds(i * 2, 2)] = blk.astype(BF).reshape(2, 4, 32, w)
        return carry

    def part_a(i, carry):
        c, w = STARTS[0], WIDTHS[0]
        blk = dot(r.xt[pl.ds(pl.multiple_of(i * 256, 256), 256), :], r.dg[:, c : c + w])
        r.pa[i // 4, lax.rem(i, 4)] = blk.astype(BF)
        return carry

    def send_x(src_of, dst):
        return [remote(src_of(lax.rem(x + o, 4)), dst.at[o - 1], x_peer(o)) for o in (1, 3, 2)]

    def send_y(src_of, dst):
        out = []
        for o in (1, 3, 2):
            t = lax.rem(y + o, 4)
            out.append(remote(src_of(lax.rem(t, 2), t // 2), dst.at[o - 1], y_peer(o)))
        return out

    def send_z(src_of, dst):
        return [remote(src_of(lax.rem(z + o, 4)), dst.at[o - 1], z_peer(o)) for o in (1, 3, 2)]

    lax.fori_loop(0, 8, part_b, 0)
    b1 = send_y(lambda lo, hi: r.pb.at[lo, :, hi], r.rb1)
    lax.fori_loop(0, 8, part_c, 0)
    c1 = send_z(lambda j: r.pc.at[:, j], r.rc1)
    lax.fori_loop(0, 8, part_a, 0)
    a1 = send_x(lambda j: r.pa.at[:, j], r.ra1)

    def mix(i, carry):
        here = pl.ds(pl.multiple_of(i * 256, 256), 256)
        there = pl.ds(pl.multiple_of(768 - i * 256, 256), 256)
        rev = dot(r.gr[256:512, there], r.jm[...])
        r.mx[:, here] = (r.gr[0:256, here].astype(F32) + rev).astype(BF)
        return carry

    lax.fori_loop(0, 4, mix, 0)
    tail_local, tail_remote = [], []
    for i in range(2):
        span = pl.ds(512 * i, 512)
        dst = mixed.at[0, :, pl.ds(offs[i], 512)]
        tail_local.append(local(r.mx.at[pl.ds(own, 128), span], dst))
        tail_remote.append(remote(r.mx.at[pl.ds(theirs, 128), span], dst, partner))

    rim_df.wait_recv()
    rim_dr.wait_recv()

    @pl.when(chip == 7)
    def _():
        r.df[256:512, :] = jnp.zeros((256, 1024), BF)

    @pl.when(chip == 0)
    def _():
        r.dr[0:256, :] = jnp.zeros((256, 1024), BF)

    sm_own = r.sm.at[0, x]
    sm_own[...] = jnp.zeros((8, SMALL), F32)

    def back_conv(g, carry):
        here = pl.ds(pl.multiple_of(g * 128, 128), 128)
        ds_f = dot(r.uu[g], r.df[:, here]).astype(BF)
        r.dsf[0:256, here] = ds_f
        ds_r = dot(r.tt[g], r.dr[:, here]).astype(BF)
        r.dsr[16:272, here] = ds_r
        lag_f = dot_nt(r.df[0:256, here], r.sf[:, here])
        r.ls[0, g] = skew_sum(lag_f, True)
        lag_r = dot_nt(r.dr[256:512, here], r.sr[:, here])
        r.ls[1, g] = skew_sum(lag_r, True)
        fwd = r.xf[:, here].astype(F32)
        rev = r.xr[:, here].astype(F32)
        ds_f32, ds_r32 = ds_f.astype(F32), ds_r.astype(F32)
        for k in range(4):
            xk = fwd[16:272] if k == 0 else pltpu.roll(fwd, k, 0)[16:272]
            rk = rev[0:256] if k == 0 else pltpu.roll(rev, 272 - k, 0)[0:256]
            sm_own[k : k + 1, here] = jnp.sum(ds_f32 * xk + ds_r32 * rk, axis=0, keepdims=True)
        return carry

    lax.fori_loop(0, 8, back_conv, 0)
    rim_dsf = remote(r.dsf.at[pl.ds(0, 16)], r.dsf.at[pl.ds(256, 16)], at_chip(prv, core))
    rim_dsr = remote(r.dsr.at[pl.ds(256, 16)], r.dsr.at[pl.ds(0, 16)], at_chip(nxt, core))

    sums = []
    for strand in range(2):
        total = r.ls[strand, :, 0, :]
        for t in range(1, 8):
            total = total + pltpu.roll(r.ls[strand, :, t, :], 512 - t, 1)
        sums.append(total)
    lag_m = lax.broadcasted_iota(jnp.int32, (512, 256), 0)
    lag_k = lax.broadcasted_iota(jnp.int32, (512, 256), 1)
    turned = jnp.dot(
        sums[0],
        jnp.where(lag_m + lag_k == 256, 1.0, 0.0),
        precision=lax.Precision.HIGHEST,
        preferred_element_type=F32,
    )
    sm_own[:, 1024:SMALL] = turned + sums[1][:, 0:256]
    small_x = [remote(r.sm.at[0, x], r.sm.at[0, x], x_peer(o)) for o in (1, 3, 2)]

    def d_input(i, carry):
        here = pl.ds(pl.multiple_of(i * 256, 256), 256)
        there = pl.ds(pl.multiple_of(1792 - i * 256, 256), 256)
        rev = dot_nt(r.dg[256:512, :], r.w[there, :]).astype(BF)
        r.dh[:, here] = dot_nt(r.dg[0:256, :], r.w[here, :]) + dot(rev, r.jm[...])
        return carry

    lax.fori_loop(0, 8, d_input, 0)

    rim_dsf.wait_recv()
    rim_dsr.wait_recv()

    @pl.when(chip == 7)
    def _():
        r.dsf[256:272, :] = jnp.zeros((16, 1024), BF)

    @pl.when(chip == 0)
    def _():
        r.dsr[0:16, :] = jnp.zeros((16, 1024), BF)

    def short_back(g, carry):
        here = pl.ds(pl.multiple_of(g * 128, 128), 128)
        there = pl.ds(col(g, 128), 128)
        fwd = r.dsf[:, here].astype(F32)
        rev = r.dsr[:, here].astype(F32)
        acc_f = r.st[0:1, there] * fwd[0:256]
        acc_r = r.st[0:1, there] * rev[16:272]
        for k in range(1, 4):
            tap = r.st[k : k + 1, there]
            acc_f += tap * pltpu.roll(fwd, 272 - k, 0)[0:256]
            acc_r += tap * pltpu.roll(rev, k, 0)[16:272]
        r.dh[:, there] = r.dh[:, there] + acc_f
        r.dxr[:, here] = acc_r.astype(BF)
        return carry

    lax.fori_loop(0, 8, short_back, 0)
    for i in range(4):
        there = pl.ds(col(i, 256), 256)
        r.dh[:, there] = r.dh[:, there] + dot(r.dxr[:, 768 - 256 * i : 1024 - 256 * i], r.jm[...])
    r.dhs[...] = r.dh[pl.ds(theirs, 128), :].astype(BF)
    pair_d = remote(r.dhs, r.dhr, partner)

    def summed(ref_own, ref_got, copies):
        for copy in copies:
            copy.wait_recv()
        total = ref_own[...].astype(F32)
        for o in range(3):
            total = total + ref_got[o].astype(F32)
        return total

    def add_stage(count_, own_at, got, copies, put):
        for copy in copies:
            copy.wait_recv()

        def step(i, carry):
            total = own_at(i).astype(F32)
            for o in range(3):
                total = total + got[o, i].astype(F32)
            put(i, total.astype(BF))
            return carry

        lax.fori_loop(0, count_, step, 0)

    def put_b1(i, v):
        r.sb1[i // 4, lax.rem(i, 4)] = v

    def put_c1(i, v):
        r.sc1[i // 8, lax.rem(i // 2, 4), pl.ds(pl.multiple_of(lax.rem(i, 2) * 32, 32), 32)] = v

    def put_a1(i, v):
        r.sa1[i] = v.reshape(8, 2, 16, WIDTHS[0])

    add_stage(32, lambda i: r.pb[y_lo, i, y_hi], r.rb1, b1, put_b1)
    b2 = send_z(lambda j: r.sb1.at[:, j], r.rb2)
    add_stage(16, lambda i: r.pc[i, z], r.rc1, c1, put_c1)
    c2 = send_x(lambda j: r.sc1.at[:, j], r.rc2)
    add_stage(2, lambda i: r.pa[i, x], r.ra1, a1, put_a1)
    a2 = send_y(lambda lo, hi: r.sa1.at[lo, :, hi], r.ra2)

    def small_sum(stage, copies):
        for copy in copies:
            copy.wait_recv()
        return (r.sm[stage, 0] + r.sm[stage, 1]) + (r.sm[stage, 2] + r.sm[stage, 3])

    r.sm[1, y] = small_sum(0, small_x)
    small_y = [remote(r.sm.at[1, y], r.sm.at[1, y], y_peer(o)) for o in (1, 3, 2)]

    pair_d.wait_recv()
    r.dho[...] = (r.dh[pl.ds(own, 128), :] + r.dhr[...].astype(F32)).astype(BF)
    tail_local.append(local(r.dho, dhid.at[0]))

    r.sb2[...] = summed(r.sb1.at[:, z], r.rb2, b2).astype(BF).reshape(4, 32, WIDTHS[1])
    b3 = send_x(lambda j: r.sb2.at[j], r.rb3)
    r.sc2[...] = summed(r.sc1.at[:, x], r.rc2, c2).astype(BF).reshape(2, 2, 2, 16, WIDTHS[2])
    c3 = send_y(lambda lo, hi: r.sc2.at[lo, :, hi], r.rc3)
    r.sa2[...] = summed(r.sa1.at[y_lo, :, y_hi], r.ra2, a2).astype(BF).reshape(2, 4, 16, WIDTHS[0])
    a3 = send_z(lambda j: r.sa2.at[:, j], r.ra3)

    r.sm[2, z] = small_sum(1, small_y)
    small_z = [remote(r.sm.at[2, z], r.sm.at[2, z], z_peer(o)) for o in (1, 3, 2)]

    def put_fin(part, value):
        r.fin[:, :, STARTS[part] : STARTS[part] + WIDTHS[part]] = value.reshape(2, 16, WIDTHS[part])

    put_fin(1, summed(r.sb2.at[x], r.rb3, b3))
    put_fin(2, summed(r.sc2.at[y_lo, :, y_hi], r.rc3, c3))
    put_fin(0, summed(r.sa2.at[:, z], r.ra3, a3))
    for i in range(2):
        span = pl.ds(512 * i, 512)
        dst = ggate.at[:, pl.ds(offs[i], 512)]
        tail_local.append(local(r.fin.at[core, :, span], dst))
        tail_remote.append(remote(r.fin.at[other, :, span], dst, partner))

    r.smo[...] = small_sum(2, small_z)
    tail_local.append(local(r.smo, small.at[core]))
    tail_remote.append(remote(r.smo, small.at[core], partner))

    for copy in tail_local:
        copy.wait()
    for copy in tail_remote:
        copy.wait_recv()
    for copy in started:
        copy.wait_send()


def body(hidden, short_taps, long_taps, gate_weight, upstream):
    outside = pl.BlockSpec(memory_space=pl.ANY)
    inside = pl.BlockSpec(memory_space=pltpu.VMEM)
    mixed, ggate, small, dhid = pl.pallas_call(
        kernel,
        out_shape=(
            jax.ShapeDtypeStruct((1, 128, 2048), BF),
            jax.ShapeDtypeStruct((16, 2048), F32),
            jax.ShapeDtypeStruct((2, 8, SMALL), F32),
            jax.ShapeDtypeStruct((1, 128, 2048), BF),
        ),
        in_specs=[outside, inside, inside, outside, outside],
        out_specs=(outside,) * 4,
        scratch_shapes=[pltpu.VMEM(shape, dtype) for shape, dtype in SCRATCH.values()]
        + [
            pltpu.SemaphoreType.DMA((LOCAL_SEMS,)),
            pltpu.SemaphoreType.DMA((REMOTE_SEMS,)),
            pltpu.SemaphoreType.DMA((REMOTE_SEMS,)),
        ],
        compiler_params=pltpu.CompilerParams(
            collective_id=0, has_side_effects=True, vmem_limit_bytes=60 * 1024 * 1024
        ),
        cost_estimate=pl.CostEstimate(
            flops=8 * 10**9, bytes_accessed=12 * 2**20, transcendentals=2**20
        ),
    )(hidden, short_taps, long_taps, gate_weight, upstream)
    edge, middle = small[1], small[0]
    grad_short = jnp.concatenate(
        [edge[0:4, 0:512], middle[0:4, 0:1024], edge[0:4, 512:1024]], axis=1
    )
    edge_lag, middle_lag = edge[:, 1024:], middle[:, 1024:]
    grad_long = jnp.transpose(jnp.concatenate([edge_lag[0:4], middle_lag, edge_lag[4:8]], axis=0))
    return (mixed, ggate, grad_short, grad_long, dhid)


def solution(mesh):
    placed = (P("dp", "seq", None), P(), P(), P(), P("dp", "seq", None))
    return jax.shard_map(
        body,
        mesh=mesh,
        in_specs=placed,
        out_specs=(P("dp", "seq", None), P(("seq", "dp"), None), P(), P(), P("dp", "seq", None)),
        check_vma=False,
    )
```

time: 890 us -> 83 us (0.09); the launches traced: 875 us -> 82.6 us
  waiting for transfers between devices: 581 us -> 0 us
  blocking collectives: 91 us -> 0 us
  local copies, waits for them, and re-layouts: 89.5 us -> 7.58 us
  Pallas kernels: 0 us -> 73.2 us
  starting transfers between devices: 54.3 us -> 0 us
  matrix products: 34.3 us -> 0 us
  between operations: 15 us -> 0.65 us
  other arithmetic: 10.4 us -> 1.24 us
    reduce_scatter x1 -> x0, waiting for transfers between devices: 467 us -> none  [body(): lax.psum_scatter(jnp.einsum('tr,tc->rc', flat_input, flat_gate, preferred...]
    ppermute x22 -> x0, waiting for transfers between devices: 114 us -> none  [the longest x16 96 us: swapped(): return lax.ppermute(block, axis, route)]
    psum x1 -> x0, blocking collectives: 91 us -> none  [body(): grad_short, grad_long = lax.psum((short_term, lag_term), ('seq', 'dp'))]
    pallas_call x0 -> x1, Pallas kernels: none -> 73.2 us  [body(): pl.pallas_call(kernel, out_shape=(jax.ShapeDtypeStruct((1, 128, 2048), BF...]
    ppermute x22 -> x0, starting transfers between devices: 54.3 us -> none  [the longest x6 27.5 us: passed_along(): lax.ppermute(value, axis, [(source, source + steps) for source in range(l...]
    dot_general x12 -> x0, matrix products: 34.3 us -> none  [the longest x6 8.55 us: band_apply(): jnp.einsum('gij,snjgc->snigc', banded[:, :, part_index * block_size:(part...]
    rev x6 -> x0, local copies, waits for them, and re-layouts: 19.6 us -> none  [the longest x1 8.76 us: body(): reverse_up = jnp.flip(far_upstream[0], (0, 1))]
    reshape x4 -> x0, local copies, waits for them, and re-layouts: 19.2 us -> none  [the longest x2 11.9 us: band_matrix(): skewed = tiled.reshape(group_count, block_size, width - 1)]
  transfers between devices with their start and end apart: 23 -> 0, of which waited for: 13 -> 0; matrix products, arithmetic and copies ran while one was open for 11% -> 0% of each run, Pallas kernels for 0% -> 0%
where the time goes in v1:
time: 83 us; the launch traced here: 82.6 us
  Pallas kernels  73.2 us (88%)
  local copies, waits for them, and re-layouts  7.58 us (9%)
  other arithmetic  1.24 us (1%)
    pallas_call x1, Pallas kernels, body(): pl.pallas_call(kernel, out_shape=(jax.ShapeDtypeStruct((1, 128, 2048), BF...  73.2 us
    unnamed x4, local copies, waits for them, and re-layouts  6.76 us

profile of v1, /device:TPU:1, one launch (start us, length us, event | category | flops | bytes accessed | tf_op | source)
XLA Modules:
  0.0 82.6 jit_solution(16177283245147889188)
XLA Ops:
  0.6 1.4 %copy.10.ltaps = bf16[256,16]{1,0:T(8,128)(2,1)} copy(bf16[256,16]{0,1:T(8,128)(2,1)} %param.7) | data formatting | bytes 16384 | tf_op args[2]
  2.1 73.2 %shard_map.92 = (bf16[1,128,2048]{2,1,0:T(8,128)(2,1)}, f32[16,2048]{1,0:T(8,128)}, f32[2,8,1280]{2,1,0:T(8,128)}, bf16[1,128,2048]{2,1,0:T(8,128)(2,1)}) custom-call(bf16[1,128,2048]{2,1,0:T(8,128)(2,1)} %hidden.1, bf16[4,2048]{1,0:T(4,128)(2,1)} %staps.1, bf16[256,16]{1,0:T(8,128)(2,1)} %copy.10.ltaps, bf16[2048,2048]{1,0:T(8,128)(2,1)} %weight.1, ...), custom_call_target="tpu_custom_call" | custom-call | flops 8000000000 | bytes 12582912 | tf_op jit(solution)/shard_map/pallas_call | solution.py:586
  75.2 0.8 slice_bitcast_fusion
  76.1 0.6 maximum_bitcast_fusion
  76.7 0.6 pad_maximum_fusion
  77.3 1.9 %copy.14 = bf16[1,128,2048]{2,1,0:T(8,128)(2,1)} copy(bf16[1,128,2048]{2,1,0:T(8,128)(2,1)} %get-tuple-element.24) | data formatting | bytes 1048576
  79.2 1.6 %copy.15 = f32[16,2048]{1,0:T(8,128)} copy(f32[16,2048]{1,0:T(8,128)} %get-tuple-element.25) | data formatting | bytes 262144
  80.7 1.9 %copy.16 = bf16[1,128,2048]{2,1,0:T(8,128)(2,1)} copy(bf16[1,128,2048]{2,1,0:T(8,128)(2,1)} %get-tuple-element.28) | data formatting | bytes 1048576
  (4 shorter events, 0.0 us)

commit v2 on v1

v2 whole, which is shorter than its diff:
```python
import types

import jax
import jax.numpy as jnp
from jax import lax
from jax.experimental import pallas as pl
from jax.experimental.pallas import tpu as pltpu
from jax.sharding import PartitionSpec as P

BF = jnp.bfloat16
F32 = jnp.float32
MESH = pl.DeviceIdType.MESH
NT = (((1,), (1,)), ((), ()))

PARTS = (("z", 0, 384), ("y", 384, 128), ("z", 768, 256), ("y", 512, 128), ("x", 640, 128))
ROUTES = dict(
    x=("xyz", (2, 4, 256), (2, 8, 2, 16), (2, 4, 16), (2, 256), (8, 16), (2, 16)),
    y=("yzx", (2, 32, 2, 16), (8, 4, 16), (4, 32), (32, 16), (8, 16), (32,)),
    z=("zxy", (16, 4, 32), (2, 4, 64), (2, 2, 2, 16), (16, 32), (2, 64), (2, 16)),
)
RING = 4
SMALL = 1280

SCRATCH = dict(
    hh=((512, 2048), BF),
    w=((2048, 1024), BF),
    up=((256, 1024), BF),
    upj=((256, 1024), BF),
    halo=((2, 16, 2048), BF),
    st=((4, 2048), F32),
    xf=((528, 1024), BF),
    xr=((528, 1024), BF),
    xn=((256, 1024), BF),
    sf=((512, 1024), BF),
    sr=((512, 1024), BF),
    df=((512, 1024), BF),
    dr=((512, 1024), BF),
    gate=((512, 1024), F32),
    gr=((512, 1024), BF),
    mx=((256, 1024), BF),
    dg=((512, 1024), BF),
    tt=((8, 256, 512), BF),
    uu=((8, 256, 512), BF),
    tv=((16, 512), F32),
    uv=((16, 512), F32),
    jm=((256, 256), BF),
    im=((256, 256), BF),
    xt=((2048, 512), BF),
    fin=((2, 16, 1024), F32),
    dsf=((272, 1024), BF),
    dsr=((272, 1024), BF),
    ls=((2, 8, 8, 512), F32),
    sm=((3, 4, 8, SMALL), F32),
    smo=((8, SMALL), F32),
    dh=((256, 2048), F32),
    dxr=((256, 1024), BF),
    dhs=((128, 2048), BF),
    dhr=((128, 2048), BF),
    dho=((128, 2048), BF),
)
for n, (axis, _, columns) in enumerate(PARTS):
    _, *layouts = ROUTES[axis]
    for m, layout in enumerate(layouts):
        copies_ = () if m < 3 else (2,) if m == 3 else (3,)
        SCRATCH[f"{'pstabc'[m]}{n}"] = (copies_ + layout + (columns,), BF)
    SCRATCH[f"r{n}"] = ((2, layouts[3][0] // 2) + layouts[3][1:] + (columns,), BF)
LOCAL_SEMS = 16
REMOTE_SEMS = 110


def dot(a, b):
    return jnp.dot(a, b, preferred_element_type=F32)


def dot_nt(a, b):
    return lax.dot_general(a, b, NT, preferred_element_type=F32)


def skew_sum(m, to_left):
    rows, lanes = m.shape
    while rows > 8:
        rows //= 2
        shift = lanes - rows if to_left else rows
        m = m[:rows] + pltpu.roll(m[rows:], shift, 1)
    return m


def kernel(hidden, staps, ltaps, weight, upstream, mixed, ggate, small, dhid, *scratch):
    r = types.SimpleNamespace(**dict(zip(SCRATCH, scratch)))
    loc, send, recv = scratch[len(SCRATCH) :]

    seq, dp = lax.axis_index("seq"), lax.axis_index("dp")
    core = lax.rem(seq, 2)
    chip = seq // 2
    x = lax.rem(chip, 4)
    y_lo = chip // 4
    y_hi = lax.rem(dp, 2)
    y = y_hi * 2 + y_lo
    z = dp // 2
    other = 1 - core

    def at_chip(c, k):
        return {"seq": c * 2 + k, "dp": dp}

    def x_peer(o):
        return {"seq": (y_lo * 4 + lax.rem(x + o, 4)) * 2 + core, "dp": dp}

    def y_peer(o):
        t = lax.rem(y + o, 4)
        return {
            "seq": (lax.rem(t, 2) * 4 + x) * 2 + core,
            "dp": z * 2 + t // 2,
        }

    def z_peer(o):
        return {"seq": seq, "dp": lax.rem(z + o, 4) * 2 + y_hi}

    partner = at_chip(chip, other)
    nxt, prv = lax.rem(chip + 1, 8), lax.rem(chip + 7, 8)
    far_chip = lax.rem(chip + 6 + 4 * core, 8)
    peers = [partner]
    peers += [at_chip(lax.rem(chip + o, 8), k) for o in (1, 7, 2, 6) for k in range(2)]
    peers += [f(o) for f in (x_peer, y_peer, z_peer) for o in (1, 2, 3)]

    offs = [pl.multiple_of(512 * other, 512), pl.multiple_of(1024 + 512 * core, 512)]
    offs_other = [pl.multiple_of(512 * core, 512), pl.multiple_of(1024 + 512 * other, 512)]
    own = pl.multiple_of(core * 128, 128)
    theirs = pl.multiple_of(other * 128, 128)

    def col(g, width):
        half = 512 // width
        c = jnp.where(g < half, 512 * other + g * width, 512 + 512 * core + g * width)
        return pl.multiple_of(c, width)

    started = []
    count = [0]

    def remote(src, dst, device, recv_index=None):
        i = count[0]
        count[0] += 1
        copy = pltpu.make_async_remote_copy(
            src_ref=src,
            dst_ref=dst,
            send_sem=send.at[i],
            recv_sem=recv.at[i if recv_index is None else recv_index],
            device_id=device,
            device_id_type=MESH,
        )
        copy.start()
        started.append(copy)
        return copy

    lcount = [0]

    def local(src, dst):
        copy = pltpu.make_async_copy(src, dst, loc.at[lcount[0]])
        lcount[0] += 1
        copy.start()
        return copy

    in_h = local(hidden.at[0], r.hh.at[pl.ds(own, 128)])
    in_u = [
        local(
            upstream.at[0, :, pl.ds(offs[i], 512)],
            r.up.at[pl.ds(own, 128), pl.ds(512 * i, 512)],
        )
        for i in range(2)
    ]
    in_w = [
        local(weight.at[:, pl.ds(offs[i], 512)], r.w.at[:, pl.ds(512 * i, 512)])
        for i in range(2)
    ]

    barrier = pltpu.get_barrier_semaphore()
    for peer in peers:
        pl.semaphore_signal(barrier, inc=1, device_id=peer, device_id_type=MESH)

    pl.semaphore_wait(barrier, len(peers))
    base = REMOTE_SEMS
    pair_h = remote(hidden.at[0], r.hh.at[pl.ds(own, 128)], partner)

    def send_rims(wave):
        for k in range(2):
            for i, span, there in ((wave, 16 + own, True), (1 - wave, own, False)):
                off = (512 * (1 - k), 1024 + 512 * k)[i]
                src = hidden.at[0, :, pl.ds(off, 512)]
                at = (pl.ds(pl.multiple_of(span, 16), 128), pl.ds(512 * i, 512))
                index = base + (0 if there else 4) + core * 2 + i
                if there:
                    remote(src, r.xf.at[at], at_chip(nxt, k), index)
                else:
                    remote(src, r.xn.at[at], at_chip(prv, k), index)

    send_rims(0)
    halo_src = hidden.at[0, pl.ds(pl.multiple_of(core * 112, 16), 16)]
    for k in range(2):
        remote(halo_src, r.halo.at[other], at_chip(far_chip, k), base + 8 + other)
    pair_u = [
        remote(
            upstream.at[0, :, pl.ds(offs_other[i], 512)],
            r.up.at[pl.ds(own, 128), pl.ds(512 * i, 512)],
            partner,
        )
        for i in range(2)
    ]

    def arrived(src, dst, i):
        pltpu.make_async_remote_copy(
            src_ref=src,
            dst_ref=dst,
            send_sem=send.at[0],
            recv_sem=recv.at[base + i],
            device_id=partner,
            device_id_type=MESH,
        ).wait_recv()

    rows_i = lax.broadcasted_iota(jnp.int32, (256, 256), 0)
    cols_i = lax.broadcasted_iota(jnp.int32, (256, 256), 1)
    r.jm[...] = jnp.where(rows_i + cols_i == 255, 1.0, 0.0).astype(BF)
    r.im[...] = jnp.where(rows_i == cols_i, 1.0, 0.0).astype(BF)
    r.st[...] = staps[...].astype(F32)

    tap_i = lax.broadcasted_iota(jnp.int32, (256, 512), 0)
    lag_i = lax.broadcasted_iota(jnp.int32, (256, 512), 1)
    taps = ltaps[...]
    r.tv[...] = dot(taps, jnp.where(tap_i + lag_i == 256, 1.0, 0.0).astype(BF))
    r.uv[...] = dot(taps, jnp.where(tap_i == lag_i, 1.0, 0.0).astype(BF))

    def toeplitz(g, carry):
        gg = col(g, 128) // 128
        for vec, out in ((r.tv, r.tt), (r.uv, r.uu)):
            first = pltpu.roll(
                jnp.broadcast_to(vec[pl.ds(gg, 1), :], (32, 512)), 0, 1, stride=1, stride_axis=0
            )
            for b in range(8):
                block = first if b == 0 else pltpu.roll(first, 32 * b, 1)
                out[g, 32 * b : 32 * b + 32, :] = block.astype(BF)
        return carry


    in_h.wait()
    pair_h.wait_recv()

    def flip_rows(i, carry):
        here = pl.multiple_of(i * 256, 256)
        there = pl.multiple_of(1792 - i * 256, 256)
        r.hh[256:512, pl.ds(here, 256)] = dot(r.hh[0:256, pl.ds(there, 256)], r.jm[...]).astype(BF)
        return carry

    lax.fori_loop(0, 8, flip_rows, 0)

    for i in range(2):
        span = slice(512 * i, 512 * i + 512)
        r.xf[272:528, span] = r.hh[0:256, pl.ds(offs[i], 512)]
        r.xr[0:256, span] = r.hh[256:512, pl.ds(offs[i], 512)]

    send_rims(1)

    def short_conv(src_f, dst_f, src_r, dst_r, count_, wave):
        def step(g, carry):
            here = pl.ds(pl.multiple_of(g * 128, 128), 128)
            there = pl.ds(col(g, 128), 128)
            fwd = r.xf[src_f : src_f + count_ + 16, here].astype(F32)
            rev = r.xr[src_r : src_r + count_ + 16, here].astype(F32)
            acc_f = r.st[0:1, there] * fwd[16:]
            acc_r = r.st[0:1, there] * rev[:count_]
            for k in range(1, 4):
                tap = r.st[k : k + 1, there]
                acc_f += tap * pltpu.roll(fwd, k, 0)[16:]
                acc_r += tap * pltpu.roll(rev, count_ + 16 - k, 0)[:count_]
            r.sf[dst_f : dst_f + count_, here] = acc_f.astype(BF)
            r.sr[dst_r : dst_r + count_, here] = acc_r.astype(BF)
            return carry

        lax.fori_loop(4 * wave, 4 * wave + 4, step, 0)

    for copy in in_w + in_u:
        copy.wait()
    for copy in pair_u:
        copy.wait_recv()

    def gate_block(i, carry):
        here = pl.ds(pl.multiple_of(i * 256, 256), 256)
        there = pl.ds(pl.multiple_of(768 - i * 256, 256), 256)
        r.gate[:, here] = dot(r.hh[...], r.w[:, here])
        r.upj[:, here] = dot(r.up[:, there], r.jm[...]).astype(BF)

        def rows(b, carry):
            at = pl.multiple_of(b * 32, 32)
            gf = r.gate[pl.ds(at, 32), here]
            gb = r.gate[pl.ds(at + 256, 32), here]
            uf = r.up[pl.ds(at, 32), here].astype(F32)
            ub = r.upj[pl.ds(at, 32), here].astype(F32)
            r.df[pl.ds(at, 32), here] = (uf * gf * jax.nn.sigmoid(gf)).astype(BF)
            r.dr[pl.ds(at + 256, 32), here] = (ub * gb * jax.nn.sigmoid(gb)).astype(BF)
            return carry

        return lax.fori_loop(0, 8, rows, carry)

    def transposed(i, carry):
        here = pl.ds(pl.multiple_of(i * 256, 256), 256)
        r.xt[here, 0:256] = dot_nt(r.im[...], r.hh[0:256, here]).astype(BF)
        r.xt[here, 256:512] = dot_nt(r.im[...], r.hh[256:512, here]).astype(BF)
        return carry

    def flip_next(i, carry):
        here = pl.ds(pl.multiple_of(i * 256, 256), 256)
        there = pl.ds(pl.multiple_of(768 - i * 256, 256), 256)
        r.xr[256:512, here] = dot(r.xn[:, there], r.jm[...]).astype(BF)
        far = r.halo[1, :, pl.ds(col(3 - i, 256), 256)]
        r.xr[512:528, here] = dot(far, r.jm[...]).astype(BF)
        return carry

    def long_conv(g, carry):
        here = pl.ds(pl.multiple_of(g * 128, 128), 128)
        for start, mat, inp, upref in ((0, r.tt, r.sf, r.up), (256, r.uu, r.sr, r.upj)):
            long_out = dot(mat[g], inp[:, here])
            g_pre = r.gate[start : start + 256, here]
            s = jax.nn.sigmoid(g_pre)
            ul = upref[:, here].astype(F32) * long_out
            r.gr[start : start + 256, here] = (g_pre * s * long_out).astype(BF)
            r.dg[start : start + 256, here] = (ul * s * (1.0 + g_pre * (1.0 - s))).astype(BF)
        return carry

    def put_term(n, i, c, blk):
        axis, start, w = PARTS[n]
        ref = getattr(r, f"p{n}")
        lo, at = i // 2, lax.rem(i, 2) * 2
        first, last = max(c, start), min(c + 256, start + w)
        blk = blk[:, first - c : last - c].astype(BF)
        span, width = pl.ds(first - start, last - first), last - first
        if axis == "x":
            ref[lo, pl.ds(at, 2), :, span] = blk.reshape(2, 256, width)
        elif axis == "y":
            ref[lo, pl.ds(at * 8, 16), :, :, span] = blk.reshape(16, 2, 16, width)
        else:
            ref[pl.ds(i * 4, 4), :, :, span] = blk.reshape(4, 4, 32, width)

    def terms(c, *parts):
        def step(i, carry):
            at = pl.ds(pl.multiple_of(i * 512, 512), 512)
            blk = dot(r.xt[at, :], r.dg[:, c : c + 256])
            for n in parts:
                put_term(n, i, c, blk)
            return carry

        lax.fori_loop(0, 4, step, 0)

    def share(axis, ref, lead, o):
        if axis == "y":
            t = lax.rem(y + o, 4)
            return ref.at[lax.rem(t, 2), :, t // 2]
        t = lax.rem((x if axis == "x" else z) + o, 4)
        return ref.at[t] if lead == 0 else ref.at[:, t]

    peer_of = dict(x=x_peer, y=y_peer, z=z_peer)

    def across(axis, ref, lead, dst):
        return [
            remote(share(axis, ref, lead, o), dst.at[o - 1], peer_of[axis](o)) for o in (1, 3, 2)
        ]

    flight = {}

    def halves(ref):
        half = ref.shape[0] // 2
        return ref.at[pl.ds(0, half)], ref.at[pl.ds(half, half)]

    def start_ring(n):
        axis = PARTS[n][0]
        term, relay, got = (getattr(r, f"{c}{n}") for c in "pra")
        ahead, behind, far = (halves(share(axis, term, 1, o)) for o in (1, 3, 2))
        got_a, got_b = halves(got.at[0]), halves(got.at[1])
        up, down = peer_of[axis](1), peer_of[axis](3)
        relays = [remote(far[0], relay.at[0], up), remote(far[1], relay.at[1], down)]
        direct = [remote(ahead[1], got_a[1], up), remote(behind[0], got_b[0], down)]
        flight[n, "relay"] = relays
        flight[n, 0] = direct

    def pass_on(n):
        axis = PARTS[n][0]
        term, relay, got = (getattr(r, f"{c}{n}") for c in "pra")
        ahead, behind = (halves(share(axis, term, 1, o)) for o in (1, 3))
        got_a, got_b = halves(got.at[0]), halves(got.at[1])
        up, down = peer_of[axis](1), peer_of[axis](3)
        for i, (held, dst, peer) in enumerate(((ahead[0], got_a[0], up), (behind[1], got_b[1], down))):
            flight[n, "relay"][i].wait_recv()
            held[...] = (held[...].astype(F32) + relay[i].astype(F32)).astype(BF)
            flight[n, 0].append(remote(held, dst, peer))

    def start_stage(n, stage):
        axis = ROUTES[PARTS[n][0]][0][stage]
        ref = getattr(r, f"{'pst'[stage]}{n}")
        lead = len(ref.shape) - 3 if stage == 2 else 1
        flight[n, stage] = across(axis, ref, lead, getattr(r, f"{'abc'[stage]}{n}"))

    def end_stage(n, stage):
        axis = ROUTES[PARTS[n][0]][0][stage]
        w = PARTS[n][2]
        for copy in flight[n, stage]:
            copy.wait_recv()
        ref = getattr(r, f"{'pst'[stage]}{n}")
        got = getattr(r, f"{'abc'[stage]}{n}")
        held = share(axis, ref, len(ref.shape) - 3 if stage == 2 else 1, 0)
        if stage == 0:
            out = getattr(r, f"s{n}")
            steps, rows = {"x": (2, 256), "y": (32, 16), "z": (16, 32)}[axis]
            batch = 256 // rows

            def step(b, carry):
                at = pl.ds(b * batch, batch)
                total = held[at].astype(F32)
                for o in range(2):
                    total = total + got[o, at].astype(F32)
                total = total.astype(BF)
                if axis == "x":
                    out[pl.ds(b, 1)] = total.reshape(1, 8, 2, 16, w)
                elif axis == "y":
                    out[pl.ds(b * 4, 4)] = total.reshape(4, 4, 16, w)
                else:
                    out[pl.ds(b, 1)] = total.reshape(1, 4, 64, w)
                return carry

            lax.fori_loop(0, 2, step, 0)
            return
        total = held[...].astype(F32)
        for o in range(3):
            total = total + got[o].astype(F32)
        if stage == 1:
            out = getattr(r, f"t{n}")
            out[...] = total.astype(BF).reshape(out.shape)
        else:
            c = PARTS[n][1]
            r.fin[:, :, c : c + w] = total.reshape(2, 16, w)

    rims_d = []
    for wave in range(2):
        half = pl.ds(512 * wave, 512)
        span = slice(512 * wave, 512 * wave + 512)
        lax.fori_loop(2 * wave, 2 * wave + 2, gate_block, 0)
        df_at, dr_at = r.df.at[pl.ds(0, 256), half], r.dr.at[pl.ds(256, 256), half]
        rims_d.append(remote(df_at, r.df.at[pl.ds(256, 256), half], at_chip(prv, core)))
        rims_d.append(remote(dr_at, r.dr.at[pl.ds(0, 256), half], at_chip(nxt, core)))
        short_conv(272, 272, 0, 0, 240, wave)
        if wave == 0:
            lax.fori_loop(0, 8, toeplitz, 0)
            lax.fori_loop(0, 8, transposed, 0)
            for k in range(2):
                arrived(halo_src, r.halo.at[k], 8 + k)
            for i in range(2):
                r.xf[0:16, 512 * i : 512 * i + 512] = r.halo[0, :, pl.ds(offs[i], 512)]
        back = pl.ds(512 * (1 - wave), 512)
        for k in range(2):
            src = hidden.at[0, :, pl.ds(0, 512)]
            arrived(src, r.xf.at[pl.ds(16 + 128 * k, 128), half], k * 2 + wave)
            arrived(src, r.xn.at[pl.ds(128 * k, 128), back], 4 + k * 2 + 1 - wave)
        lax.fori_loop(2 * wave, 2 * wave + 2, flip_next, 0)

        @pl.when(chip == 0)
        def _():
            r.xf[0:272, span] = jnp.zeros((272, 512), BF)

        @pl.when(chip == 1)
        def _():
            r.xf[0:16, span] = jnp.zeros((16, 512), BF)

        @pl.when(chip == 7)
        def _():
            r.xr[256:528, span] = jnp.zeros((272, 512), BF)

        @pl.when(chip == 6)
        def _():
            r.xr[512:528, span] = jnp.zeros((16, 512), BF)

        short_conv(0, 0, 240, 240, 272, wave)
        lax.fori_loop(4 * wave, 4 * wave + 4, long_conv, 0)
        for c in ((0, 256), (768, 512))[wave]:
            terms(c, *[n for n, (_, b, w) in enumerate(PARTS) if b < c + 256 and c < b + w])
            for n in {256: (0, 1), 768: (2,), 512: (3, 4)}.get(c, ()):
                start_ring(n)
    for n in (0, 1):
        pass_on(n)

    def mix(i, carry):
        here = pl.ds(pl.multiple_of(i * 256, 256), 256)
        there = pl.ds(pl.multiple_of(768 - i * 256, 256), 256)
        rev = dot(r.gr[256:512, there], r.jm[...])
        r.mx[:, here] = (r.gr[0:256, here].astype(F32) + rev).astype(BF)
        return carry

    lax.fori_loop(0, 4, mix, 0)
    tail_local, tail_remote = [], []
    for i in range(2):
        span = pl.ds(512 * i, 512)
        dst = mixed.at[0, :, pl.ds(offs[i], 512)]
        tail_local.append(local(r.mx.at[pl.ds(own, 128), span], dst))
        tail_remote.append(remote(r.mx.at[pl.ds(theirs, 128), span], dst, partner))

    for n in (2, 3, 4):
        pass_on(n)
    for n in (0, 1):
        end_stage(n, 0)
        start_stage(n, 1)

    for copy in rims_d:
        copy.wait_recv()

    @pl.when(chip == 7)
    def _():
        r.df[256:512, :] = jnp.zeros((256, 1024), BF)

    @pl.when(chip == 0)
    def _():
        r.dr[0:256, :] = jnp.zeros((256, 1024), BF)

    sm_own = r.sm.at[0, x]
    sm_own[...] = jnp.zeros((8, SMALL), F32)

    def back_conv(g, carry):
        here = pl.ds(pl.multiple_of(g * 128, 128), 128)
        ds_f = dot(r.uu[g], r.df[:, here]).astype(BF)
        r.dsf[0:256, here] = ds_f
        ds_r = dot(r.tt[g], r.dr[:, here]).astype(BF)
        r.dsr[16:272, here] = ds_r
        lag_f = dot_nt(r.df[0:256, here], r.sf[:, here])
        r.ls[0, g] = skew_sum(lag_f, True)
        lag_r = dot_nt(r.dr[256:512, here], r.sr[:, here])
        r.ls[1, g] = skew_sum(lag_r, True)
        fwd = r.xf[256:528, here].astype(F32)
        rev = r.xr[0:272, here].astype(F32)
        ds_f32, ds_r32 = ds_f.astype(F32), ds_r.astype(F32)
        for k in range(4):
            xk = fwd[16:272] if k == 0 else pltpu.roll(fwd, k, 0)[16:272]
            rk = rev[0:256] if k == 0 else pltpu.roll(rev, 272 - k, 0)[0:256]
            sm_own[k : k + 1, here] = jnp.sum(ds_f32 * xk + ds_r32 * rk, axis=0, keepdims=True)
        return carry

    lax.fori_loop(0, 8, back_conv, 0)
    rim_dsf = remote(r.dsf.at[pl.ds(0, 16)], r.dsf.at[pl.ds(256, 16)], at_chip(prv, core))
    rim_dsr = remote(r.dsr.at[pl.ds(256, 16)], r.dsr.at[pl.ds(0, 16)], at_chip(nxt, core))

    sums = []
    for strand in range(2):
        total = r.ls[strand, :, 0, :]
        for t in range(1, 8):
            total = total + pltpu.roll(r.ls[strand, :, t, :], 512 - t, 1)
        sums.append(total)
    lag_m = lax.broadcasted_iota(jnp.int32, (512, 256), 0)
    lag_k = lax.broadcasted_iota(jnp.int32, (512, 256), 1)
    turned = jnp.dot(
        sums[0],
        jnp.where(lag_m + lag_k == 256, 1.0, 0.0),
        precision=lax.Precision.HIGHEST,
        preferred_element_type=F32,
    )
    sm_own[:, 1024:SMALL] = turned + sums[1][:, 0:256]
    small_x = [remote(r.sm.at[0, x], r.sm.at[0, x], x_peer(o)) for o in (1, 3, 2)]

    for n in (2, 3, 4):
        end_stage(n, 0)
        start_stage(n, 1)
    for n in (0, 1):
        end_stage(n, 1)
        start_stage(n, 2)

    def small_sum(stage, copies):
        for copy in copies:
            copy.wait_recv()
        return (r.sm[stage, 0] + r.sm[stage, 1]) + (r.sm[stage, 2] + r.sm[stage, 3])

    r.sm[1, y] = small_sum(0, small_x)
    small_y = [remote(r.sm.at[1, y], r.sm.at[1, y], y_peer(o)) for o in (1, 3, 2)]

    def d_input(i, carry):
        here = pl.ds(pl.multiple_of(i * 256, 256), 256)
        there = pl.ds(pl.multiple_of(1792 - i * 256, 256), 256)
        rev = dot_nt(r.dg[256:512, :], r.w[there, :]).astype(BF)
        r.dh[:, here] = dot_nt(r.dg[0:256, :], r.w[here, :]) + dot(rev, r.jm[...])
        return carry

    lax.fori_loop(0, 4, d_input, 0)
    for n in (2, 3, 4):
        end_stage(n, 1)
        start_stage(n, 2)
    r.sm[2, z] = small_sum(1, small_y)
    small_z = [remote(r.sm.at[2, z], r.sm.at[2, z], z_peer(o)) for o in (1, 3, 2)]
    lax.fori_loop(4, 8, d_input, 0)

    rim_dsf.wait_recv()
    rim_dsr.wait_recv()

    @pl.when(chip == 7)
    def _():
        r.dsf[256:272, :] = jnp.zeros((16, 1024), BF)

    @pl.when(chip == 0)
    def _():
        r.dsr[0:16, :] = jnp.zeros((16, 1024), BF)

    def short_back(g, carry):
        here = pl.ds(pl.multiple_of(g * 128, 128), 128)
        there = pl.ds(col(g, 128), 128)
        fwd = r.dsf[:, here].astype(F32)
        rev = r.dsr[:, here].astype(F32)
        acc_f = r.st[0:1, there] * fwd[0:256]
        acc_r = r.st[0:1, there] * rev[16:272]
        for k in range(1, 4):
            tap = r.st[k : k + 1, there]
            acc_f += tap * pltpu.roll(fwd, 272 - k, 0)[0:256]
            acc_r += tap * pltpu.roll(rev, k, 0)[16:272]
        r.dh[:, there] = r.dh[:, there] + acc_f
        r.dxr[:, here] = acc_r.astype(BF)
        return carry

    lax.fori_loop(0, 8, short_back, 0)
    for i in range(4):
        there = pl.ds(col(i, 256), 256)
        r.dh[:, there] = r.dh[:, there] + dot(r.dxr[:, 768 - 256 * i : 1024 - 256 * i], r.jm[...])
    r.dhs[...] = r.dh[pl.ds(theirs, 128), :].astype(BF)
    pair_d = remote(r.dhs, r.dhr, partner)

    pair_d.wait_recv()
    r.dho[...] = (r.dh[pl.ds(own, 128), :] + r.dhr[...].astype(F32)).astype(BF)
    tail_local.append(local(r.dho, dhid.at[0]))
    for n in range(5):
        end_stage(n, 2)
    for i in range(2):
        span = pl.ds(512 * i, 512)
        dst = ggate.at[:, pl.ds(offs[i], 512)]
        tail_local.append(local(r.fin.at[core, :, span], dst))
        tail_remote.append(remote(r.fin.at[other, :, span], dst, partner))

    r.smo[...] = small_sum(2, small_z)
    tail_local.append(local(r.smo, small.at[core]))
    tail_remote.append(remote(r.smo, small.at[core], partner))

    for copy in tail_local:
        copy.wait()
    for copy in tail_remote:
        copy.wait_recv()
    for copy in started:
        copy.wait_send()


def finish(mixed, ggate, small, dhid, mixed_out, ggate_out, dhid_out, short_out, long_out, *rest):
    sems = rest[-1]
    held = rest[:3]
    reads = [
        pltpu.make_async_copy(src, dst, sems.at[i])
        for i, (src, dst) in enumerate(zip((mixed, dhid, ggate), held))
    ]
    writes = [
        pltpu.make_async_copy(src, dst, sems.at[3 + i])
        for i, (src, dst) in enumerate(zip(held, (mixed_out, dhid_out, ggate_out)))
    ]
    small_v = rest[3]
    read_small = pltpu.make_async_copy(small, small_v, sems.at[6])
    read_small.start()
    for copy in reads:
        copy.start()
    read_small.wait()
    small = small_v
    short_out[:, 0:512] = small[1, 0:4, 0:512]
    short_out[:, 512:1536] = small[0, 0:4, 0:1024]
    short_out[:, 1536:2048] = small[1, 0:4, 512:1024]
    long_out[0:4, :] = small[1, 0:4, 1024:SMALL]
    long_out[4:12, :] = small[0, :, 1024:SMALL]
    long_out[12:16, :] = small[1, 4:8, 1024:SMALL]
    for read, write in zip(reads, writes):
        read.wait()
        write.start()
    for write in writes:
        write.wait()


def body(hidden, short_taps, long_taps, gate_weight, upstream):
    outside = pl.BlockSpec(memory_space=pl.ANY)
    inside = pl.BlockSpec(memory_space=pltpu.VMEM)
    block = jax.ShapeDtypeStruct((1, 128, 2048), BF)
    gate_rows = jax.ShapeDtypeStruct((16, 2048), F32)
    mixed, ggate, small, dhid = pl.pallas_call(
        kernel,
        out_shape=(block, gate_rows, jax.ShapeDtypeStruct((2, 8, SMALL), F32), block),
        in_specs=[outside, inside, inside, outside, outside],
        out_specs=(outside,) * 4,
        scratch_shapes=[pltpu.VMEM(shape, dtype) for shape, dtype in SCRATCH.values()]
        + [
            pltpu.SemaphoreType.DMA((LOCAL_SEMS,)),
            pltpu.SemaphoreType.DMA((REMOTE_SEMS,)),
            pltpu.SemaphoreType.DMA((REMOTE_SEMS + 10,)),
        ],
        compiler_params=pltpu.CompilerParams(
            collective_id=0, has_side_effects=True, vmem_limit_bytes=60 * 1024 * 1024
        ),
        cost_estimate=pl.CostEstimate(
            flops=8 * 10**9, bytes_accessed=12 * 2**20, transcendentals=2**20
        ),
    )(hidden, short_taps, jnp.transpose(long_taps), gate_weight, upstream)
    mixed, ggate, dhid, grad_short, grad_long = pl.pallas_call(
        finish,
        out_shape=(
            block,
            gate_rows,
            block,
            jax.ShapeDtypeStruct((4, 2048), F32),
            jax.ShapeDtypeStruct((16, 256), F32),
        ),
        in_specs=[outside] * 4,
        out_specs=(outside, outside, outside, inside, inside),
        scratch_shapes=[
            pltpu.VMEM((1, 128, 2048), BF),
            pltpu.VMEM((1, 128, 2048), BF),
            pltpu.VMEM((16, 2048), F32),
            pltpu.VMEM((2, 8, SMALL), F32),
            pltpu.SemaphoreType.DMA((7,)),
        ],
        compiler_params=pltpu.CompilerParams(vmem_limit_bytes=60 * 1024 * 1024),
    )(mixed, ggate, small, dhid)
    return (mixed, ggate, grad_short, jnp.transpose(grad_long), dhid)


def solution(mesh):
    placed = (P("dp", "seq", None), P(), P(), P(), P("dp", "seq", None))
    return jax.shard_map(
        body,
        mesh=mesh,
        in_specs=placed,
        out_specs=(P("dp", "seq", None), P(("seq", "dp"), None), P(), P(), P("dp", "seq", None)),
        check_vma=False,
    )
```

time: 83 us -> 76.8 us (0.925)
  local copies, waits for them, and re-layouts: 7.58 us -> 0 us
  Pallas kernels: 73.2 us -> 75.9 us
  other arithmetic: 1.24 us -> 0 us
    unnamed x4 -> x0, local copies, waits for them, and re-layouts: 6.76 us -> none
    pallas_call x1 -> x2, Pallas kernels: 73.2 us -> 75.9 us  [the longest x1 73.1 us: body(): pl.pallas_call(kernel, out_shape=(block, gate_rows, jax.ShapeDtypeStruct(...]
where the time goes in v2:
time: 76.8 us; the launch traced here: 76.5 us
  Pallas kernels  75.9 us (99%)
    pallas_call x1, Pallas kernels, body(): pl.pallas_call(kernel, out_shape=(block, gate_rows, jax.ShapeDtypeStruct(...  73.1 us
    pallas_call x1, Pallas kernels, body(): pl.pallas_call(finish, out_shape=(block, gate_rows, block, jax.ShapeDtype...  2.77 us

profile of v2, /device:TPU:1, one launch (start us, length us, event | category | flops | bytes accessed | tf_op | source)
XLA Modules:
  0.0 76.5 jit_solution(17084045553573302902)
XLA Ops:
  0.6 73.1 %shard_map.92 = (bf16[1,128,2048]{2,1,0:T(8,128)(2,1)}, f32[16,2048]{1,0:T(8,128)}, f32[2,8,1280]{2,1,0:T(8,128)}, bf16[1,128,2048]{2,1,0:T(8,128)(2,1)}) custom-call(bf16[1,128,2048]{2,1,0:T(8,128)(2,1)} %hidden.1, bf16[4,2048]{1,0:T(4,128)(2,1)} %staps.1, bf16[16,256]{1,0:T(8,128)(2,1)} %bitcast.3, bf16[2048,2048]{1,0:T(8,128)(2,1)} %weight.1, ...), custom_call_target="tpu_custom_call" | custom-call | flops 8000000000 | bytes 12582912 | tf_op jit(solution)/shard_map/pallas_call | solution.py:681
  73.8 2.8 %shard_map.93 = (bf16[1,128,2048]{2,1,0:T(8,128)(2,1)}, f32[16,2048]{1,0:T(8,128)}, bf16[1,128,2048]{2,1,0:T(8,128)(2,1)}, f32[4,2048]{1,0:T(4,128)}, f32[16,256]{1,0:T(8,128)}) custom-call(bf16[1,128,2048]{2,1,0:T(8,128)(2,1)} %get-tuple-element.14.mixed, f32[16,2048]{1,0:T(8,128)} %get-tuple-element.15.ggate, f32[2,8,1280]{2,1,0:T(8,128)} %get-tuple-element.16.small, ...), custom_call_target="tpu_custom_call" | custom-call | tf_op jit(solution)/shard_map/pallas_call | solution.py:699

commit v3 on v2

--- a/solution.py
+++ b/solution.py
@@ -19,7 +19,7 @@
     z=("zxy", (16, 4, 32), (2, 4, 64), (2, 2, 2, 16), (16, 32), (2, 64), (2, 16)),
 )
 RING = 4
-SMALL = 1280
+SMALL = 768
 
 SCRATCH = dict(
     hh=((512, 2048), BF),
@@ -496,27 +496,10 @@
         tail_local.append(local(r.mx.at[pl.ds(own, 128), span], dst))
         tail_remote.append(remote(r.mx.at[pl.ds(theirs, 128), span], dst, partner))
 
-    for n in (2, 3, 4):
-        pass_on(n)
-    for n in (0, 1):
-        end_stage(n, 0)
-        start_stage(n, 1)
-
-    for copy in rims_d:
-        copy.wait_recv()
-
-    @pl.when(chip == 7)
-    def _():
-        r.df[256:512, :] = jnp.zeros((256, 1024), BF)
-
-    @pl.when(chip == 0)
-    def _():
-        r.dr[0:256, :] = jnp.zeros((256, 1024), BF)
-
-    sm_own = r.sm.at[0, x]
-    sm_own[...] = jnp.zeros((8, SMALL), F32)
-
-    def back_conv(g, carry):
+    sm_own = r.sm.at[0, z]
+
+    def back_conv(wave, g, carry):
+        row, spot = 4 * wave, pl.ds(pl.multiple_of((g - 4 * wave) * 128, 128), 128)
         here = pl.ds(pl.multiple_of(g * 128, 128), 128)
         ds_f = dot(r.uu[g], r.df[:, here]).astype(BF)
         r.dsf[0:256, here] = ds_f
@@ -532,10 +515,54 @@
         for k in range(4):
             xk = fwd[16:272] if k == 0 else pltpu.roll(fwd, k, 0)[16:272]
             rk = rev[0:256] if k == 0 else pltpu.roll(rev, 272 - k, 0)[0:256]
-            sm_own[k : k + 1, here] = jnp.sum(ds_f32 * xk + ds_r32 * rk, axis=0, keepdims=True)
-        return carry
-
-    lax.fori_loop(0, 8, back_conv, 0)
+            total = jnp.sum(ds_f32 * xk + ds_r32 * rk, axis=0, keepdims=True)
+            sm_own[row + k : row + k + 1, spot] = total
+        return carry
+
+    def d_input(i, carry):
+        here = pl.ds(pl.multiple_of(i * 256, 256), 256)
+        there = pl.ds(pl.multiple_of(1792 - i * 256, 256), 256)
+        rev = dot_nt(r.dg[256:512, :], r.w[there, :]).astype(BF)
+        r.dh[:, here] = dot_nt(r.dg[0:256, :], r.w[here, :]) + dot(rev, r.jm[...])
+        return carry
+
+    def rims_of(wave):
+        span = slice(512 * wave, 512 * wave + 512)
+        for copy in rims_d[2 * wave : 2 * wave + 2]:
+            copy.wait_recv()
+
+        @pl.when(chip == 7)
+        def _():
+            r.df[256:512, span] = jnp.zeros((256, 512), BF)
+
+        @pl.when(chip == 0)
+        def _():
+            r.dr[0:256, span] = jnp.zeros((256, 512), BF)
+
+    def stages(parts, stage):
+        for n in parts:
+            end_stage(n, stage)
+            start_stage(n, stage + 1)
+
+    small_axes = ((z, z_peer), (y, y_peer), (x, x_peer))
+
+    def small_send(stage):
+        at, peer = small_axes[stage]
+        return [remote(r.sm.at[stage, at], r.sm.at[stage, at], peer(o)) for o in (1, 3, 2)]
+
+    def small_sum(stage, copies):
+        for copy in copies:
+            copy.wait_recv()
+        return (r.sm[stage, 0] + r.sm[stage, 1]) + (r.sm[stage, 2] + r.sm[stage, 3])
+
+    rims_of(0)
+    lax.fori_loop(0, 4, lambda g, carry: back_conv(0, g, carry), 0)
+    lax.fori_loop(0, 4, d_input, 0)
+    for n in (2, 3, 4):
+        pass_on(n)
+    stages((0, 1), 0)
+    rims_of(1)
+    lax.fori_loop(4, 8, lambda g, carry: back_conv(1, g, carry), 0)
     rim_dsf = remote(r.dsf.at[pl.ds(0, 16)], r.dsf.at[pl.ds(256, 16)], at_chip(prv, core))
     rim_dsr = remote(r.dsr.at[pl.ds(256, 16)], r.dsr.at[pl.ds(0, 16)], at_chip(nxt, core))
 
@@ -553,38 +580,14 @@
         precision=lax.Precision.HIGHEST,
         preferred_element_type=F32,
     )
-    sm_own[:, 1024:SMALL] = turned + sums[1][:, 0:256]
-    small_x = [remote(r.sm.at[0, x], r.sm.at[0, x], x_peer(o)) for o in (1, 3, 2)]
-
-    for n in (2, 3, 4):
-        end_stage(n, 0)
-        start_stage(n, 1)
-    for n in (0, 1):
-        end_stage(n, 1)
-        start_stage(n, 2)
-
-    def small_sum(stage, copies):
-        for copy in copies:
-            copy.wait_recv()
-        return (r.sm[stage, 0] + r.sm[stage, 1]) + (r.sm[stage, 2] + r.sm[stage, 3])
-
-    r.sm[1, y] = small_sum(0, small_x)
-    small_y = [remote(r.sm.at[1, y], r.sm.at[1, y], y_peer(o)) for o in (1, 3, 2)]
-
-    def d_input(i, carry):
-        here = pl.ds(pl.multiple_of(i * 256, 256), 256)
-        there = pl.ds(pl.multiple_of(1792 - i * 256, 256), 256)
-        rev = dot_nt(r.dg[256:512, :], r.w[there, :]).astype(BF)
-        r.dh[:, here] = dot_nt(r.dg[0:256, :], r.w[here, :]) + dot(rev, r.jm[...])
-        return carry
-
-    lax.fori_loop(0, 4, d_input, 0)
-    for n in (2, 3, 4):
-        end_stage(n, 1)
-        start_stage(n, 2)
-    r.sm[2, z] = small_sum(1, small_y)
-    small_z = [remote(r.sm.at[2, z], r.sm.at[2, z], z_peer(o)) for o in (1, 3, 2)]
-    lax.fori_loop(4, 8, d_input, 0)
+    sm_own[:, 512:SMALL] = turned + sums[1][:, 0:256]
+    small_0 = small_send(0)
+    stages((2, 3, 4), 0)
+    lax.fori_loop(4, 6, d_input, 0)
+    r.sm[1, y] = small_sum(0, small_0)
+    small_1 = small_send(1)
+    stages((0, 1), 1)
+    lax.fori_loop(6, 8, d_input, 0)
 
     rim_dsf.wait_recv()
     rim_dsr.wait_recv()
@@ -619,6 +622,10 @@
     r.dhs[...] = r.dh[pl.ds(theirs, 128), :].astype(BF)
     pair_d = remote(r.dhs, r.dhr, partner)
 
+    r.sm[2, x] = small_sum(1, small_1)
+    small_2 = small_send(2)
+    stages((2, 3, 4), 1)
+
     pair_d.wait_recv()
     r.dho[...] = (r.dh[pl.ds(own, 128), :] + r.dhr[...].astype(F32)).astype(BF)
     tail_local.append(local(r.dho, dhid.at[0]))
@@ -630,7 +637,7 @@
         tail_local.append(local(r.fin.at[core, :, span], dst))
         tail_remote.append(remote(r.fin.at[other, :, span], dst, partner))
 
-    r.smo[...] = small_sum(2, small_z)
+    r.smo[...] = small_sum(2, small_2)
     tail_local.append(local(r.smo, small.at[core]))
     tail_remote.append(remote(r.smo, small.at[core], partner))
 
@@ -660,12 +667,11 @@
         copy.start()
     read_small.wait()
     small = small_v
-    short_out[:, 0:512] = small[1, 0:4, 0:512]
-    short_out[:, 512:1536] = small[0, 0:4, 0:1024]
-    short_out[:, 1536:2048] = small[1, 0:4, 512:1024]
-    long_out[0:4, :] = small[1, 0:4, 1024:SMALL]
-    long_out[4:12, :] = small[0, :, 1024:SMALL]
-    long_out[12:16, :] = small[1, 4:8, 1024:SMALL]
+    for i, (half, row) in enumerate(((1, 0), (0, 0), (0, 4), (1, 4))):
+        short_out[:, 512 * i : 512 * i + 512] = small[half, row : row + 4, 0:512]
+    long_out[0:4, :] = small[1, 0:4, 512:SMALL]
+    long_out[4:12, :] = small[0, :, 512:SMALL]
+    long_out[12:16, :] = small[1, 4:8, 512:SMALL]
     for read, write in zip(reads, writes):
         read.wait()
         write.start()

time: 76.8 us -> 70 us (0.911)
  Pallas kernels: 75.9 us -> 69.1 us
    pallas_call x1, Pallas kernels: 73.1 us -> 66.3 us  [body(): pl.pallas_call(kernel, out_shape=(block, gate_rows, jax.ShapeDtypeStruct(...]
where the time goes in v3:
time: 70 us; the launch traced here: 69.7 us
  Pallas kernels  69.1 us (99%)
    pallas_call x1, Pallas kernels, body(): pl.pallas_call(kernel, out_shape=(block, gate_rows, jax.ShapeDtypeStruct(...  66.3 us
    pallas_call x1, Pallas kernels, body(): pl.pallas_call(finish, out_shape=(block, gate_rows, block, jax.ShapeDtype...  2.75 us

profile of v3, /device:TPU:1, one launch (start us, length us, event | category | flops | bytes accessed | tf_op | source)
XLA Modules:
  0.0 69.7 jit_solution(9529981937960693805)
XLA Ops:
  0.6 66.3 %shard_map.92 = (bf16[1,128,2048]{2,1,0:T(8,128)(2,1)}, f32[16,2048]{1,0:T(8,128)}, f32[2,8,768]{2,1,0:T(8,128)}, bf16[1,128,2048]{2,1,0:T(8,128)(2,1)}) custom-call(bf16[1,128,2048]{2,1,0:T(8,128)(2,1)} %hidden.1, bf16[4,2048]{1,0:T(4,128)(2,1)} %staps.1, bf16[16,256]{1,0:T(8,128)(2,1)} %bitcast.3, bf16[2048,2048]{1,0:T(8,128)(2,1)} %weight.1, ...), custom_call_target="tpu_custom_call" | custom-call | flops 8000000000 | bytes 12582912 | tf_op jit(solution)/shard_map/pallas_call | solution.py:687
  67.0 2.7 %shard_map.93 = (bf16[1,128,2048]{2,1,0:T(8,128)(2,1)}, f32[16,2048]{1,0:T(8,128)}, bf16[1,128,2048]{2,1,0:T(8,128)(2,1)}, f32[4,2048]{1,0:T(4,128)}, f32[16,256]{1,0:T(8,128)}) custom-call(bf16[1,128,2048]{2,1,0:T(8,128)(2,1)} %get-tuple-element.14.mixed, f32[16,2048]{1,0:T(8,128)} %get-tuple-element.15.ggate, f32[2,8,768]{2,1,0:T(8,128)} %get-tuple-element.16.small, ...), custom_call_target="tpu_custom_call" | custom-call | tf_op jit(solution)/shard_map/pallas_call | solution.py:705

commit v4 on v3

--- a/solution.py
+++ b/solution.py
@@ -12,7 +12,9 @@
 MESH = pl.DeviceIdType.MESH
 NT = (((1,), (1,)), ((), ()))
 
-PARTS = (("z", 0, 384), ("y", 384, 128), ("z", 768, 256), ("y", 512, 128), ("x", 640, 128))
+PARTS = (("z", 0, 512, True), ("x", 768, 256, False), ("y", 512, 256, False))
+EARLY = (0,)
+LATE = tuple(range(1, len(PARTS)))
 ROUTES = dict(
     x=("xyz", (2, 4, 256), (2, 8, 2, 16), (2, 4, 16), (2, 256), (8, 16), (2, 16)),
     y=("yzx", (2, 32, 2, 16), (8, 4, 16), (4, 32), (32, 16), (8, 16), (32,)),
@@ -53,17 +55,19 @@
     sm=((3, 4, 8, SMALL), F32),
     smo=((8, SMALL), F32),
     dh=((256, 2048), F32),
+    dv=((256, 2048), BF),
     dxr=((256, 1024), BF),
     dhs=((128, 2048), BF),
     dhr=((128, 2048), BF),
     dho=((128, 2048), BF),
 )
-for n, (axis, _, columns) in enumerate(PARTS):
+for n, (axis, _, columns, ring) in enumerate(PARTS):
     _, *layouts = ROUTES[axis]
     for m, layout in enumerate(layouts):
-        copies_ = () if m < 3 else (2,) if m == 3 else (3,)
+        copies_ = () if m < 3 else (2,) if m == 3 and ring else (3,)
         SCRATCH[f"{'pstabc'[m]}{n}"] = (copies_ + layout + (columns,), BF)
-    SCRATCH[f"r{n}"] = ((2, layouts[3][0] // 2) + layouts[3][1:] + (columns,), BF)
+    if ring:
+        SCRATCH[f"r{n}"] = ((2, layouts[3][0] // 2) + layouts[3][1:] + (columns,), BF)
 LOCAL_SEMS = 16
 REMOTE_SEMS = 110
 
@@ -238,6 +242,7 @@
         return carry
 
 
+    lax.fori_loop(0, 8, toeplitz, 0)
     in_h.wait()
     pair_h.wait_recv()
 
@@ -295,12 +300,17 @@
             r.dr[pl.ds(at + 256, 32), here] = (ub * gb * jax.nn.sigmoid(gb)).astype(BF)
             return carry
 
-        return lax.fori_loop(0, 8, rows, carry)
+        return lax.fori_loop(0, 8, rows, carry, unroll=4)
 
     def transposed(i, carry):
         here = pl.ds(pl.multiple_of(i * 256, 256), 256)
         r.xt[here, 0:256] = dot_nt(r.im[...], r.hh[0:256, here]).astype(BF)
-        r.xt[here, 256:512] = dot_nt(r.im[...], r.hh[256:512, here]).astype(BF)
+        return carry
+
+    def transposed_flip(i, carry):
+        here = pl.ds(pl.multiple_of(i * 256, 256), 256)
+        there = pl.ds(pl.multiple_of(1792 - i * 256, 256), 256)
+        r.xt[here, 256:512] = dot(r.jm[...], r.xt[there, 0:256]).astype(BF)
         return carry
 
     def flip_next(i, carry):
@@ -323,7 +333,7 @@
         return carry
 
     def put_term(n, i, c, blk):
-        axis, start, w = PARTS[n]
+        axis, start, w, _ = PARTS[n]
         ref = getattr(r, f"p{n}")
         lo, at = i // 2, lax.rem(i, 2) * 2
         first, last = max(c, start), min(c + 256, start + w)
@@ -368,6 +378,9 @@
 
     def start_ring(n):
         axis = PARTS[n][0]
+        if not PARTS[n][3]:
+            start_stage(n, 0)
+            return
         term, relay, got = (getattr(r, f"{c}{n}") for c in "pra")
         ahead, behind, far = (halves(share(axis, term, 1, o)) for o in (1, 3, 2))
         got_a, got_b = halves(got.at[0]), halves(got.at[1])
@@ -379,6 +392,8 @@
 
     def pass_on(n):
         axis = PARTS[n][0]
+        if not PARTS[n][3]:
+            return
         term, relay, got = (getattr(r, f"{c}{n}") for c in "pra")
         ahead, behind = (halves(share(axis, term, 1, o)) for o in (1, 3))
         got_a, got_b = halves(got.at[0]), halves(got.at[1])
@@ -410,7 +425,7 @@
             def step(b, carry):
                 at = pl.ds(b * batch, batch)
                 total = held[at].astype(F32)
-                for o in range(2):
+                for o in range(got.shape[0]):
                     total = total + got[o, at].astype(F32)
                 total = total.astype(BF)
                 if axis == "x":
@@ -436,15 +451,17 @@
     rims_d = []
     for wave in range(2):
         half = pl.ds(512 * wave, 512)
-        span = slice(512 * wave, 512 * wave + 512)
         lax.fori_loop(2 * wave, 2 * wave + 2, gate_block, 0)
         df_at, dr_at = r.df.at[pl.ds(0, 256), half], r.dr.at[pl.ds(256, 256), half]
         rims_d.append(remote(df_at, r.df.at[pl.ds(256, 256), half], at_chip(prv, core)))
         rims_d.append(remote(dr_at, r.dr.at[pl.ds(0, 256), half], at_chip(nxt, core)))
+    for wave in range(2):
+        half = pl.ds(512 * wave, 512)
+        span = slice(512 * wave, 512 * wave + 512)
         short_conv(272, 272, 0, 0, 240, wave)
         if wave == 0:
-            lax.fori_loop(0, 8, toeplitz, 0)
             lax.fori_loop(0, 8, transposed, 0)
+            lax.fori_loop(0, 8, transposed_flip, 0)
             for k in range(2):
                 arrived(halo_src, r.halo.at[k], 8 + k)
             for i in range(2):
@@ -475,10 +492,10 @@
         short_conv(0, 0, 240, 240, 272, wave)
         lax.fori_loop(4 * wave, 4 * wave + 4, long_conv, 0)
         for c in ((0, 256), (768, 512))[wave]:
-            terms(c, *[n for n, (_, b, w) in enumerate(PARTS) if b < c + 256 and c < b + w])
-            for n in {256: (0, 1), 768: (2,), 512: (3, 4)}.get(c, ()):
+            terms(c, *[n for n, (_, b, w, _) in enumerate(PARTS) if b < c + 256 and c < b + w])
+            for n in {256: EARLY, 768: LATE[:1], 512: LATE[1:]}.get(c, ()):
                 start_ring(n)
-    for n in (0, 1):
+    for n in EARLY:
         pass_on(n)
 
     def mix(i, carry):
@@ -521,9 +538,15 @@
 
     def d_input(i, carry):
         here = pl.ds(pl.multiple_of(i * 256, 256), 256)
+        both = dot_nt(r.dg[...], r.w[here, :])
+        r.dh[:, here] = both[0:256]
+        r.dv[:, here] = both[256:512].astype(BF)
+        return carry
+
+    def turn_back(i, carry):
+        here = pl.ds(pl.multiple_of(i * 256, 256), 256)
         there = pl.ds(pl.multiple_of(1792 - i * 256, 256), 256)
-        rev = dot_nt(r.dg[256:512, :], r.w[there, :]).astype(BF)
-        r.dh[:, here] = dot_nt(r.dg[0:256, :], r.w[here, :]) + dot(rev, r.jm[...])
+        r.dh[:, here] = r.dh[:, here] + dot(r.dv[:, there], r.jm[...])
         return carry
 
     def rims_of(wave):
@@ -558,9 +581,8 @@
     rims_of(0)
     lax.fori_loop(0, 4, lambda g, carry: back_conv(0, g, carry), 0)
     lax.fori_loop(0, 4, d_input, 0)
-    for n in (2, 3, 4):
+    for n in LATE:
         pass_on(n)
-    stages((0, 1), 0)
     rims_of(1)
     lax.fori_loop(4, 8, lambda g, carry: back_conv(1, g, carry), 0)
     rim_dsf = remote(r.dsf.at[pl.ds(0, 16)], r.dsf.at[pl.ds(256, 16)], at_chip(prv, core))
@@ -582,12 +604,17 @@
     )
     sm_own[:, 512:SMALL] = turned + sums[1][:, 0:256]
     small_0 = small_send(0)
-    stages((2, 3, 4), 0)
+    stages(EARLY, 0)
+    stages(LATE, 0)
     lax.fori_loop(4, 6, d_input, 0)
     r.sm[1, y] = small_sum(0, small_0)
     small_1 = small_send(1)
-    stages((0, 1), 1)
+    stages(EARLY, 1)
     lax.fori_loop(6, 8, d_input, 0)
+    r.sm[2, x] = small_sum(1, small_1)
+    small_2 = small_send(2)
+    stages(LATE, 1)
+    lax.fori_loop(0, 8, turn_back, 0)
 
     rim_dsf.wait_recv()
     rim_dsr.wait_recv()
@@ -622,14 +649,10 @@
     r.dhs[...] = r.dh[pl.ds(theirs, 128), :].astype(BF)
     pair_d = remote(r.dhs, r.dhr, partner)
 
-    r.sm[2, x] = small_sum(1, small_1)
-    small_2 = small_send(2)
-    stages((2, 3, 4), 1)
-
     pair_d.wait_recv()
     r.dho[...] = (r.dh[pl.ds(own, 128), :] + r.dhr[...].astype(F32)).astype(BF)
     tail_local.append(local(r.dho, dhid.at[0]))
-    for n in range(5):
+    for n in range(len(PARTS)):
         end_stage(n, 2)
     for i in range(2):
         span = pl.ds(512 * i, 512)

time: 70 us -> 67.5 us (0.964)
  Pallas kernels: 69.1 us -> 66.6 us
    pallas_call x1, Pallas kernels: 66.3 us -> 63.9 us  [body(): pl.pallas_call(kernel, out_shape=(block, gate_rows, jax.ShapeDtypeStruct(...]
where the time goes in v4:
time: 67.5 us; the launch traced here: 67.2 us
  Pallas kernels  66.6 us (99%)
    pallas_call x1, Pallas kernels, body(): pl.pallas_call(kernel, out_shape=(block, gate_rows, jax.ShapeDtypeStruct(...  63.9 us
    pallas_call x1, Pallas kernels, body(): pl.pallas_call(finish, out_shape=(block, gate_rows, block, jax.ShapeDtype...  2.75 us

profile of v4, /device:TPU:1, one launch (start us, length us, event | category | flops | bytes accessed | tf_op | source)
XLA Modules:
  0.0 67.2 jit_solution(4148277177619582691)
XLA Ops:
  0.6 63.9 %shard_map.92 = (bf16[1,128,2048]{2,1,0:T(8,128)(2,1)}, f32[16,2048]{1,0:T(8,128)}, f32[2,8,768]{2,1,0:T(8,128)}, bf16[1,128,2048]{2,1,0:T(8,128)(2,1)}) custom-call(bf16[1,128,2048]{2,1,0:T(8,128)(2,1)} %hidden.1, bf16[4,2048]{1,0:T(4,128)(2,1)} %staps.1, bf16[16,256]{1,0:T(8,128)(2,1)} %bitcast.3, bf16[2048,2048]{1,0:T(8,128)(2,1)} %weight.1, ...), custom_call_target="tpu_custom_call" | custom-call | flops 8000000000 | bytes 12582912 | tf_op jit(solution)/shard_map/pallas_call | solution.py:710
  64.5 2.7 %shard_map.93 = (bf16[1,128,2048]{2,1,0:T(8,128)(2,1)}, f32[16,2048]{1,0:T(8,128)}, bf16[1,128,2048]{2,1,0:T(8,128)(2,1)}, f32[4,2048]{1,0:T(4,128)}, f32[16,256]{1,0:T(8,128)}) custom-call(bf16[1,128,2048]{2,1,0:T(8,128)(2,1)} %get-tuple-element.14.mixed, f32[16,2048]{1,0:T(8,128)} %get-tuple-element.15.ggate, f32[2,8,768]{2,1,0:T(8,128)} %get-tuple-element.16.small, ...), custom_call_target="tpu_custom_call" | custom-call | tf_op jit(solution)/shard_map/pallas_call | solution.py:728

commit v5 on v4

--- a/solution.py
+++ b/solution.py
@@ -12,9 +12,9 @@
 MESH = pl.DeviceIdType.MESH
 NT = (((1,), (1,)), ((), ()))
 
-PARTS = (("z", 0, 512, True), ("x", 768, 256, False), ("y", 512, 256, False))
-EARLY = (0,)
-LATE = tuple(range(1, len(PARTS)))
+PARTS = (("z", 0, 256, True), ("z", 256, 256, True), ("y", 768, 256, True), ("x", 512, 256, True))
+EARLY = (0, 1)
+LATE = tuple(range(2, len(PARTS)))
 ROUTES = dict(
     x=("xyz", (2, 4, 256), (2, 8, 2, 16), (2, 4, 16), (2, 256), (8, 16), (2, 16)),
     y=("yzx", (2, 32, 2, 16), (8, 4, 16), (4, 32), (32, 16), (8, 16), (32,)),
@@ -493,7 +493,7 @@
         lax.fori_loop(4 * wave, 4 * wave + 4, long_conv, 0)
         for c in ((0, 256), (768, 512))[wave]:
             terms(c, *[n for n, (_, b, w, _) in enumerate(PARTS) if b < c + 256 and c < b + w])
-            for n in {256: EARLY, 768: LATE[:1], 512: LATE[1:]}.get(c, ()):
+            for n in {0: EARLY[:1], 256: EARLY[1:], 768: LATE[:1], 512: LATE[1:]}.get(c, ()):
                 start_ring(n)
     for n in EARLY:
         pass_on(n)

time: 67.5 us -> 66 us (0.978)
  Pallas kernels: 66.6 us -> 65.1 us
    pallas_call x1, Pallas kernels: 63.9 us -> 62.4 us  [body(): pl.pallas_call(kernel, out_shape=(block, gate_rows, jax.ShapeDtypeStruct(...]
where the time goes in v5:
time: 66 us; the launch traced here: 65.8 us
  Pallas kernels  65.1 us (99%)
    pallas_call x1, Pallas kernels, body(): pl.pallas_call(kernel, out_shape=(block, gate_rows, jax.ShapeDtypeStruct(...  62.4 us
    pallas_call x1, Pallas kernels, body(): pl.pallas_call(finish, out_shape=(block, gate_rows, block, jax.ShapeDtype...  2.75 us

profile of v5, /device:TPU:1, one launch (start us, length us, event | category | flops | bytes accessed | tf_op | source)
XLA Modules:
  0.0 65.8 jit_solution(612882747547497970)
XLA Ops:
  0.6 62.4 %shard_map.92 = (bf16[1,128,2048]{2,1,0:T(8,128)(2,1)}, f32[16,2048]{1,0:T(8,128)}, f32[2,8,768]{2,1,0:T(8,128)}, bf16[1,128,2048]{2,1,0:T(8,128)(2,1)}) custom-call(bf16[1,128,2048]{2,1,0:T(8,128)(2,1)} %hidden.1, bf16[4,2048]{1,0:T(4,128)(2,1)} %staps.1, bf16[16,256]{1,0:T(8,128)(2,1)} %bitcast.3, bf16[2048,2048]{1,0:T(8,128)(2,1)} %weight.1, ...), custom_call_target="tpu_custom_call" | custom-call | flops 8000000000 | bytes 12582912 | tf_op jit(solution)/shard_map/pallas_call | solution.py:710
  63.0 2.7 %shard_map.93 = (bf16[1,128,2048]{2,1,0:T(8,128)(2,1)}, f32[16,2048]{1,0:T(8,128)}, bf16[1,128,2048]{2,1,0:T(8,128)(2,1)}, f32[4,2048]{1,0:T(4,128)}, f32[16,256]{1,0:T(8,128)}) custom-call(bf16[1,128,2048]{2,1,0:T(8,128)(2,1)} %get-tuple-element.14.mixed, f32[16,2048]{1,0:T(8,128)} %get-tuple-element.15.ggate, f32[2,8,768]{2,1,0:T(8,128)} %get-tuple-element.16.small, ...), custom_call_target="tpu_custom_call" | custom-call | tf_op jit(solution)/shard_map/pallas_call | solution.py:728
